TPU v7x, 32 devices: a whole 2x2x4 slice. The times are simulated.
32 devices in a mesh: dp: 8 (over y, x, core), tensor: 4 (over z).
Axes of the slice: x: 2, y: 2, z: 4, core: 2. Of those that a mesh axis runs over, the one named last changes fastest.
Arguments:
- hidden: bfloat16 [4096, 8192], P(('dp', 'tensor')), may hold values from -6 to 6
- norm_gain: float32 [8192], replicated, may hold values from 0.5 to 1.5
- tile_values: bfloat16 [4, 80, 128, 128], P('tensor', 'dp'), may hold values from -0.15625 to 0.15625
- tile_ids: int32 [4, 80], P('tensor', 'dp'), may hold values from 0 to 1279, as said below
- tile_counts: int32 [4, 8], P('tensor', 'dp'), may hold values from 5 to 10, as said below
- proj_grad: bfloat16 [4096, 10240], P('dp', 'tensor'), may hold values from -6 to 6
Outputs:
- projections: bfloat16 [4096, 10240], P('dp', 'tensor')
- hidden_grad: bfloat16 [4096, 8192], P(('dp', 'tensor'))
- tile_grads: float32 [4, 80, 128, 128], P('tensor', 'dp')
- gain_grad: float32 [8192], replicated
Inputs may be any that keep to these rules, and one draw needn't show every extreme that they name: `tile_ids`: within each tensor index the 80 block numbers are distinct; a slot's number holds whether or not the slot is live. `tile_counts`: for every tensor index some owner has all 10 slots live.
All inputs are finite; a program needn't handle non-finite values.
Results may differ from a plain program's by a relative error of at most 0.013.
Values may be sent and summed in bfloat16 or wider, within the bound.
A program may use at most 192 MiB of HBM per device.

v0:
```python
import math

import jax
import jax.numpy as jnp
from jax import lax
from jax.sharding import PartitionSpec as P

EPSILON = 1e-05


def normalize(source, norm_gain):
    source_f = source.astype(jnp.float32)
    inverse = lax.rsqrt(jnp.mean(source_f * source_f, axis=-1, keepdims=True) + EPSILON)
    return (source_f, inverse, (source_f * inverse * norm_gain).astype(jnp.bfloat16))


def selector(block_names, total_count):
    return (block_names[:, None] == jnp.arange(total_count, dtype=jnp.int32)[None, :]).astype(
        jnp.bfloat16
    )


def pick_tiles(blocks, block_names, total_count):
    chooser = selector(block_names, total_count)
    return jnp.einsum("nri,sr->nsi", blocks, chooser, preferred_element_type=jnp.float32).astype(
        jnp.bfloat16
    )


def place_tiles(values, block_names, total_count):
    chooser = selector(block_names, total_count)
    upper_half = values.astype(jnp.bfloat16)
    lower_half = (values - upper_half.astype(jnp.float32)).astype(jnp.bfloat16)
    placed = jnp.einsum("nsi,sr->nri", upper_half, chooser, preferred_element_type=jnp.float32)
    return placed + jnp.einsum(
        "nsi,sr->nri", lower_half, chooser, preferred_element_type=jnp.float32
    )


def over_groups(handler, running, tile_block, tile_names, anchor, slot_count):
    group_total = tile_names.shape[0] // slot_count

    def loop_step(group_idx, state):
        offset = group_idx * slot_count
        block_vals = lax.dynamic_slice_in_dim(tile_block, offset, slot_count, 0)
        block_names = lax.dynamic_slice_in_dim(tile_names, offset, slot_count, 0)
        return handler(state, block_vals, block_names, anchor + offset)

    return lax.fori_loop(0, group_total, loop_step, running)


def body(hidden, norm_gain, tile_values, tile_ids, tile_counts, proj_grad):
    model_width = hidden.shape[1]
    tile_size = tile_values.shape[-1]
    slot_count = tile_values.shape[1]
    seq_rows = proj_grad.shape[0]
    col_tiles = proj_grad.shape[1] // tile_size
    row_tiles = model_width // tile_size
    live_mask = (jnp.arange(slot_count) < tile_counts[0, 0]).astype(jnp.bfloat16)
    masked = tile_values[0] * live_mask[:, None, None]
    own_names = tile_ids[0]
    hidden_f, inverse, normed = normalize(hidden, norm_gain)
    gathered = lax.all_gather(normed, "tensor", axis=0, tiled=True)
    x_blocks = gathered.reshape(seq_rows, row_tiles, tile_size)
    g_blocks = proj_grad.reshape(seq_rows, col_tiles, tile_size)

    def forward_group(running, block_vals, block_names, offset):
        picked = pick_tiles(x_blocks, block_names // col_tiles, row_tiles)
        parts = jnp.einsum("nsi,sij->nsj", picked, block_vals, preferred_element_type=jnp.float32)
        return running + place_tiles(parts, block_names % col_tiles, col_tiles)

    start_out = jnp.zeros((seq_rows, col_tiles, tile_size), jnp.float32)
    all_vals, all_names = (
        lax.all_gather(masked, "dp", axis=0, tiled=True),
        lax.all_gather(own_names, "dp", axis=0, tiled=True),
    )
    outputs = over_groups(forward_group, start_out, all_vals, all_names, 0, slot_count)
    projections = outputs.reshape(seq_rows, col_tiles * tile_size).astype(jnp.bfloat16)
    slot_total_all = all_names.shape[0]

    def row_grad_of(g_part):

        def backward_group(local_grad, block_vals, block_names, offset):
            picked_g = pick_tiles(g_part, block_names % col_tiles, col_tiles)
            backward = jnp.einsum(
                "nsj,sij->nsi", picked_g, block_vals, preferred_element_type=jnp.float32
            )
            return local_grad + place_tiles(backward, block_names // col_tiles, row_tiles)

        start_grad = jnp.zeros((g_part.shape[0], row_tiles, tile_size), jnp.float32)
        local_grad = over_groups(backward_group, start_grad, all_vals, all_names, 0, slot_count)
        return local_grad.reshape(g_part.shape[0], model_width).astype(jnp.bfloat16)

    def tile_grad_of(weight_grad, x_part, g_part):

        def tile_group(tile_acc, block_vals, block_names, offset):
            picked_x = pick_tiles(x_part, block_names // col_tiles, row_tiles)
            picked_g = pick_tiles(g_part, block_names % col_tiles, col_tiles)
            tile_part = jnp.einsum(
                "nsi,nsj->sij", picked_x, picked_g, preferred_element_type=jnp.float32
            )
            current = lax.dynamic_slice_in_dim(tile_acc, offset, tile_part.shape[0], 0)
            return lax.dynamic_update_slice_in_dim(tile_acc, current + tile_part, offset, 0)

        return over_groups(tile_group, weight_grad, all_vals, all_names, 0, slot_count)

    block_rows = math.gcd(seq_rows, 256)
    start_tiles = jnp.zeros((slot_total_all, tile_size, tile_size), jnp.float32)

    def row_block(block_idx, state):
        row_grad, weight_grad = state
        begin = block_idx * block_rows
        x_part = lax.dynamic_slice_in_dim(x_blocks, begin, block_rows, 0)
        g_part = lax.dynamic_slice_in_dim(g_blocks, begin, block_rows, 0)
        rounded = row_grad_of(g_part)
        row_grad = lax.dynamic_update_slice_in_dim(row_grad, rounded, begin, 0)
        weight_grad = tile_grad_of(weight_grad, x_part, g_part)
        return (row_grad, weight_grad)

    initial_back = (jnp.zeros((seq_rows, model_width), jnp.bfloat16), start_tiles)
    row_grad, weight_grad = lax.fori_loop(0, seq_rows // block_rows, row_block, initial_back)
    row_sum = lax.psum_scatter(row_grad, "tensor", scatter_dimension=0, tiled=True).astype(
        jnp.float32
    )
    tile_sum = lax.psum_scatter(
        weight_grad.astype(jnp.bfloat16), "dp", scatter_dimension=0, tiled=True
    ).astype(jnp.float32)
    tile_grads = (tile_sum * live_mask.astype(jnp.float32)[:, None, None])[None]
    unit = hidden_f * inverse
    gain_part = jnp.sum(row_sum * unit, axis=0)
    gain_grad = lax.psum(gain_part, ("dp", "tensor"))
    scaled = row_sum * norm_gain
    hidden_grad = (
        inverse * (scaled - unit * jnp.mean(scaled * unit, axis=-1, keepdims=True))
    ).astype(jnp.bfloat16)
    return (projections, hidden_grad, tile_grads, gain_grad)


def solution(mesh):
    in_specs = (
        P(("dp", "tensor"), None),
        P(),
        P("tensor", "dp", None, None),
        P("tensor", "dp"),
        P("tensor", "dp"),
        P("dp", "tensor"),
    )
    out_specs = (P("dp", "tensor"), P(("dp", "tensor"), None), P("tensor", "dp", None, None), P())
    return jax.shard_map(body, mesh=mesh, in_specs=in_specs, out_specs=out_specs, check_vma=False)
```

profile of v0, /device:TPU:0, one launch (start us, length us, event | category | flops | bytes accessed | tf_op | source)
XLA Modules:
  0.0 951.3 jit_solution(16404277503629230293)
XLA Ops:
  20.3 9.5 all-reduce
  29.8 135.6 %all-gather.6.cloned.1.call-done = bf16[512,8192]{1,0:T(8,128)(2,1)} async-done(((bf16[128,8192]{1,0:T(8,128)(2,1)}), bf16[512,8192]{1,0:T(8,128)(2,1)}) %all-gather.6.cloned.1.call-update) | async-done | bytes 8388624 | tf_op jit(solution)/shard_map/all_gather | solution.py:63
  165.4 9.4 copy.42
  174.7 21.4 %all-gather.4.cloned.1.call-done = bf16[80,128,128]{2,1,0:T(8,128)(2,1)} async-done(((bf16[10,128,128]{2,1,0:T(8,128)(2,1)}), bf16[80,128,128]{2,1,0:T(8,128)(2,1)}) %all-gather.4.cloned.1.call-update) | async-done | bytes 2621456 | tf_op jit(solution)/shard_map/all_gather | solution.py:74
  203.4 463.0 %while.101 = (s32[]{:T(128)}, bf16[512,8192]{1,0:T(8,128)(2,1)}, f32[80,128,128]{2,1,0:T(8,128)}, bf16[512,20,128]{0,2,1:T(8,128)(2,1)}, s32[80]{0:T(128)S(1)}, ...) while((s32[]{:T(128)}, bf16[512,8192]{1,0:T(8,128)(2,1)}, ...), condition=%wide.region_8.9_spmd, body=%wide.region_3.8_spmd.sunk | while | flops 330664448 | bytes 85787744 | solution.py:121
  205.9 162.2 %while.103 = (s32[]{:T(128)}, f32[256,64,128]{2,1,0:T(8,128)}, s32[80]{0:T(128)S(1)}, bf16[80,128,128]{2,1,0:T(8,128)(2,1)}, bf16[256,20,128]{2,1,0:T(8,128)(2,1...) while((s32[]{:T(128)}, f32[256,64,128]{2,1,0:T(8,128)}, s32[80]{0:T(128)S(1)}, ...), condition=%wide.region_5.5_spmd.clone, body=%wide.region_4.4_spmd.clone.sunk | while | flops 188810816 | bytes 41746828 | solution.py:49
  216.1 8.0 bitcast_add_fusion.5
  228.7 4.6 fusion.97
  234.3 10.4 %bitcast_add_fusion.5 = f32[256,64,128]{2,1,0:T(8,128)} fusion(f32[256,64,128]{2,1,0:T(8,128)} %get-tuple-element.990, f32[64,256,128]{2,0,1:T(8,128)} %fusion.97, pred[]{:T(512)S(6)} %compare.7, bf16[256,10,128]{2,1,0:T(8,128)(2,1)S(1)} %copy.73, s32[10]{0:T(128)S(1)} %get-tuple-element.971), kind=kOutput, calls=%fused_computation.16.clone.1 | convolution fusion | flops 48235136 | bytes 25821224 | tf_op jit(solution)/shard_map/while/body/eval_jaxpr/while/body/eval_jaxpr/nsi,sr->nri/dot_general | solution.py:35
  249.3 4.6 fusion.97
  254.8 10.4 %bitcast_add_fusion.5 = f32[256,64,128]{2,1,0:T(8,128)} fusion(f32[256,64,128]{2,1,0:T(8,128)} %get-tuple-element.990, f32[64,256,128]{2,0,1:T(8,128)} %fusion.97, pred[]{:T(512)S(6)} %compare.7, bf16[256,10,128]{2,1,0:T(8,128)(2,1)S(1)} %copy.73, s32[10]{0:T(128)S(1)} %get-tuple-element.971), kind=kOutput, calls=%fused_computation.16.clone.1 | convolution fusion | flops 48235136 | bytes 25821224 | tf_op jit(solution)/shard_map/while/body/eval_jaxpr/while/body/eval_jaxpr/nsi,sr->nri/dot_general | solution.py:35
  275.4 10.4 %bitcast_add_fusion.5 = f32[256,64,128]{2,1,0:T(8,128)} fusion(f32[256,64,128]{2,1,0:T(8,128)} %get-tuple-element.990, f32[64,256,128]{2,0,1:T(8,128)} %fusion.97, pred[]{:T(512)S(6)} %compare.7, bf16[256,10,128]{2,1,0:T(8,128)(2,1)S(1)} %copy.73, s32[10]{0:T(128)S(1)} %get-tuple-element.971), kind=kOutput, calls=%fused_computation.16.clone.1 | convolution fusion | flops 48235136 | bytes 25821224 | tf_op jit(solution)/shard_map/while/body/eval_jaxpr/while/body/eval_jaxpr/nsi,sr->nri/dot_general | solution.py:35
  290.4 4.6 fusion.97
  296.0 10.4 %bitcast_add_fusion.5 = f32[256,64,128]{2,1,0:T(8,128)} fusion(f32[256,64,128]{2,1,0:T(8,128)} %get-tuple-element.990, f32[64,256,128]{2,0,1:T(8,128)} %fusion.97, pred[]{:T(512)S(6)} %compare.7, bf16[256,10,128]{2,1,0:T(8,128)(2,1)S(1)} %copy.73, s32[10]{0:T(128)S(1)} %get-tuple-element.971), kind=kOutput, calls=%fused_computation.16.clone.1 | convolution fusion | flops 48235136 | bytes 25821224 | tf_op jit(solution)/shard_map/while/body/eval_jaxpr/while/body/eval_jaxpr/nsi,sr->nri/dot_general | solution.py:35
  311.0 4.6 fusion.97
  316.5 10.4 %bitcast_add_fusion.5 = f32[256,64,128]{2,1,0:T(8,128)} fusion(f32[256,64,128]{2,1,0:T(8,128)} %get-tuple-element.990, f32[64,256,128]{2,0,1:T(8,128)} %fusion.97, pred[]{:T(512)S(6)} %compare.7, bf16[256,10,128]{2,1,0:T(8,128)(2,1)S(1)} %copy.73, s32[10]{0:T(128)S(1)} %get-tuple-element.971), kind=kOutput, calls=%fused_computation.16.clone.1 | convolution fusion | flops 48235136 | bytes 25821224 | tf_op jit(solution)/shard_map/while/body/eval_jaxpr/while/body/eval_jaxpr/nsi,sr->nri/dot_general | solution.py:35
  331.5 4.6 fusion.97
  337.1 10.4 %bitcast_add_fusion.5 = f32[256,64,128]{2,1,0:T(8,128)} fusion(f32[256,64,128]{2,1,0:T(8,128)} %get-tuple-element.990, f32[64,256,128]{2,0,1:T(8,128)} %fusion.97, pred[]{:T(512)S(6)} %compare.7, bf16[256,10,128]{2,1,0:T(8,128)(2,1)S(1)} %copy.73, s32[10]{0:T(128)S(1)} %get-tuple-element.971), kind=kOutput, calls=%fused_computation.16.clone.1 | convolution fusion | flops 48235136 | bytes 25821224 | tf_op jit(solution)/shard_map/while/body/eval_jaxpr/while/body/eval_jaxpr/nsi,sr->nri/dot_general | solution.py:35
  352.1 4.6 fusion.97
  357.7 10.4 %bitcast_add_fusion.5 = f32[256,64,128]{2,1,0:T(8,128)} fusion(f32[256,64,128]{2,1,0:T(8,128)} %get-tuple-element.990, f32[64,256,128]{2,0,1:T(8,128)} %fusion.97, pred[]{:T(512)S(6)} %compare.7, bf16[256,10,128]{2,1,0:T(8,128)(2,1)S(1)} %copy.73, s32[10]{0:T(128)S(1)} %get-tuple-element.971), kind=kOutput, calls=%fused_computation.16.clone.1 | convolution fusion | flops 48235136 | bytes 25821224 | tf_op jit(solution)/shard_map/while/body/eval_jaxpr/while/body/eval_jaxpr/nsi,sr->nri/dot_general | solution.py:35
  372.5 10.0 %bitcast_dynamic-update-slice_fusion.3 = bf16[512,8192]{1,0:T(8,128)(2,1)} fusion(bf16[512,8192]{1,0:T(8,128)(2,1)} %get-tuple-element.1081, s32[]{:T(128)S(6)} %select_n.148, bf16[32,8,64,128]{3,2,1,0:T(8,128)(2,1)S(1)} %bitcast.116), kind=kLoop, calls=%fused_computation.34.clone.1 | loop fusion | bytes 8388612 | tf_op jit(solution)/shard_map/while/body/eval_jaxpr/dynamic_update_slice | solution.py:116
  382.6 5.2 constant_dynamic-slice_fusion.5
  387.7 47.1 %while.104 = (s32[]{:T(128)}, f32[80,128,128]{2,1,0:T(8,128)}, s32[80]{0:T(128)S(1)}, bf16[256,64,128]{2,1,0:T(8,128)(2,1)}, bf16[256,20,128]{2,1,0:T(8,128)(2,1...) while((s32[]{:T(128)}, f32[80,128,128]{2,1,0:T(8,128)}, s32[80]{0:T(128)S(1)}, ...), condition=%wide.region_7.7_spmd, body=%wide.region_6.6_spmd.sunk | while | flops 139756480 | bytes 9437531 | solution.py:49
  437.4 162.2 %while.103 = (s32[]{:T(128)}, f32[256,64,128]{2,1,0:T(8,128)}, s32[80]{0:T(128)S(1)}, bf16[80,128,128]{2,1,0:T(8,128)(2,1)}, bf16[256,20,128]{2,1,0:T(8,128)(2,1...) while((s32[]{:T(128)}, f32[256,64,128]{2,1,0:T(8,128)}, s32[80]{0:T(128)S(1)}, ...), condition=%wide.region_5.5_spmd.clone, body=%wide.region_4.4_spmd.clone.sunk | while | flops 188810816 | bytes 41746828 | solution.py:49
  447.6 8.0 bitcast_add_fusion.5
  465.7 10.4 %bitcast_add_fusion.5 = f32[256,64,128]{2,1,0:T(8,128)} fusion(f32[256,64,128]{2,1,0:T(8,128)} %get-tuple-element.990, f32[64,256,128]{2,0,1:T(8,128)} %fusion.97, pred[]{:T(512)S(6)} %compare.7, bf16[256,10,128]{2,1,0:T(8,128)(2,1)S(1)} %copy.73, s32[10]{0:T(128)S(1)} %get-tuple-element.971), kind=kOutput, calls=%fused_computation.16.clone.1 | convolution fusion | flops 48235136 | bytes 25821224 | tf_op jit(solution)/shard_map/while/body/eval_jaxpr/while/body/eval_jaxpr/nsi,sr->nri/dot_general | solution.py:35
  486.3 10.4 %bitcast_add_fusion.5 = f32[256,64,128]{2,1,0:T(8,128)} fusion(f32[256,64,128]{2,1,0:T(8,128)} %get-tuple-element.990, f32[64,256,128]{2,0,1:T(8,128)} %fusion.97, pred[]{:T(512)S(6)} %compare.7, bf16[256,10,128]{2,1,0:T(8,128)(2,1)S(1)} %copy.73, s32[10]{0:T(128)S(1)} %get-tuple-element.971), kind=kOutput, calls=%fused_computation.16.clone.1 | convolution fusion | flops 48235136 | bytes 25821224 | tf_op jit(solution)/shard_map/while/body/eval_jaxpr/while/body/eval_jaxpr/nsi,sr->nri/dot_general | solution.py:35
  506.9 10.4 %bitcast_add_fusion.5 = f32[256,64,128]{2,1,0:T(8,128)} fusion(f32[256,64,128]{2,1,0:T(8,128)} %get-tuple-element.990, f32[64,256,128]{2,0,1:T(8,128)} %fusion.97, pred[]{:T(512)S(6)} %compare.7, bf16[256,10,128]{2,1,0:T(8,128)(2,1)S(1)} %copy.73, s32[10]{0:T(128)S(1)} %get-tuple-element.971), kind=kOutput, calls=%fused_computation.16.clone.1 | convolution fusion | flops 48235136 | bytes 25821224 | tf_op jit(solution)/shard_map/while/body/eval_jaxpr/while/body/eval_jaxpr/nsi,sr->nri/dot_general | solution.py:35
  527.4 10.4 %bitcast_add_fusion.5 = f32[256,64,128]{2,1,0:T(8,128)} fusion(f32[256,64,128]{2,1,0:T(8,128)} %get-tuple-element.990, f32[64,256,128]{2,0,1:T(8,128)} %fusion.97, pred[]{:T(512)S(6)} %compare.7, bf16[256,10,128]{2,1,0:T(8,128)(2,1)S(1)} %copy.73, s32[10]{0:T(128)S(1)} %get-tuple-element.971), kind=kOutput, calls=%fused_computation.16.clone.1 | convolution fusion | flops 48235136 | bytes 25821224 | tf_op jit(solution)/shard_map/while/body/eval_jaxpr/while/body/eval_jaxpr/nsi,sr->nri/dot_general | solution.py:35
  548.0 10.4 %bitcast_add_fusion.5 = f32[256,64,128]{2,1,0:T(8,128)} fusion(f32[256,64,128]{2,1,0:T(8,128)} %get-tuple-element.990, f32[64,256,128]{2,0,1:T(8,128)} %fusion.97, pred[]{:T(512)S(6)} %compare.7, bf16[256,10,128]{2,1,0:T(8,128)(2,1)S(1)} %copy.73, s32[10]{0:T(128)S(1)} %get-tuple-element.971), kind=kOutput, calls=%fused_computation.16.clone.1 | convolution fusion | flops 48235136 | bytes 25821224 | tf_op jit(solution)/shard_map/while/body/eval_jaxpr/while/body/eval_jaxpr/nsi,sr->nri/dot_general | solution.py:35
  568.6 10.4 %bitcast_add_fusion.5 = f32[256,64,128]{2,1,0:T(8,128)} fusion(f32[256,64,128]{2,1,0:T(8,128)} %get-tuple-element.990, f32[64,256,128]{2,0,1:T(8,128)} %fusion.97, pred[]{:T(512)S(6)} %compare.7, bf16[256,10,128]{2,1,0:T(8,128)(2,1)S(1)} %copy.73, s32[10]{0:T(128)S(1)} %get-tuple-element.971), kind=kOutput, calls=%fused_computation.16.clone.1 | convolution fusion | flops 48235136 | bytes 25821224 | tf_op jit(solution)/shard_map/while/body/eval_jaxpr/while/body/eval_jaxpr/nsi,sr->nri/dot_general | solution.py:35
  589.1 10.4 %bitcast_add_fusion.5 = f32[256,64,128]{2,1,0:T(8,128)} fusion(f32[256,64,128]{2,1,0:T(8,128)} %get-tuple-element.990, f32[64,256,128]{2,0,1:T(8,128)} %fusion.97, pred[]{:T(512)S(6)} %compare.7, bf16[256,10,128]{2,1,0:T(8,128)(2,1)S(1)} %copy.73, s32[10]{0:T(128)S(1)} %get-tuple-element.971), kind=kOutput, calls=%fused_computation.16.clone.1 | convolution fusion | flops 48235136 | bytes 25821224 | tf_op jit(solution)/shard_map/while/body/eval_jaxpr/while/body/eval_jaxpr/nsi,sr->nri/dot_general | solution.py:35
  604.0 10.1 %bitcast_dynamic-update-slice_fusion.3 = bf16[512,8192]{1,0:T(8,128)(2,1)} fusion(bf16[512,8192]{1,0:T(8,128)(2,1)} %get-tuple-element.1081, s32[]{:T(128)S(6)} %select_n.148, bf16[32,8,64,128]{3,2,1,0:T(8,128)(2,1)S(1)} %bitcast.116), kind=kLoop, calls=%fused_computation.34.clone.1 | loop fusion | bytes 8388612 | tf_op jit(solution)/shard_map/while/body/eval_jaxpr/dynamic_update_slice | solution.py:116
  614.1 5.2 constant_dynamic-slice_fusion.5
  619.2 47.1 %while.104 = (s32[]{:T(128)}, f32[80,128,128]{2,1,0:T(8,128)}, s32[80]{0:T(128)S(1)}, bf16[256,64,128]{2,1,0:T(8,128)(2,1)}, bf16[256,20,128]{2,1,0:T(8,128)(2,1...) while((s32[]{:T(128)}, f32[80,128,128]{2,1,0:T(8,128)}, s32[80]{0:T(128)S(1)}, ...), condition=%wide.region_7.7_spmd, body=%wide.region_6.6_spmd.sunk | while | flops 139756480 | bytes 9437531 | solution.py:49
  666.3 4.6 convert_element_type.186
  671.5 213.0 %while.102 = (s32[]{:T(128)}, f32[512,20,128]{2,1,0:T(8,128)}, s32[80]{0:T(128)S(1)}, bf16[80,128,128]{2,1,0:T(8,128)(2,1)}, bf16[512,64,128]{2,1,0:T(8,128)(2,1...) while((s32[]{:T(128)}, f32[512,20,128]{2,1,0:T(8,128)}, s32[80]{0:T(128)S(1)}, ...), condition=%wide.region_2.3_spmd.clone, body=%wide.region_1.2_spmd.clone.sunk | while | flops 311297152 | bytes 42795404 | solution.py:49
  671.6 4.6 convert_bitcast_fusion.2
  681.1 5.4 fusion.89
  689.4 7.4 bitcast_add_fusion.4
  697.0 4.7 convert_bitcast_fusion.2
  706.5 5.3 fusion.89
  714.7 9.2 bitcast_add_fusion.4
  724.0 4.6 convert_bitcast_fusion.2
  733.5 5.3 fusion.89
  741.7 9.0 bitcast_add_fusion.4
  750.8 4.7 convert_bitcast_fusion.2
  760.3 5.3 fusion.89
  768.5 9.0 bitcast_add_fusion.4
  777.5 4.7 convert_bitcast_fusion.2
  787.0 5.4 fusion.89
  795.3 9.0 bitcast_add_fusion.4
  804.4 4.7 convert_bitcast_fusion.2
  813.9 5.3 fusion.89
  822.2 9.0 bitcast_add_fusion.4
  831.2 4.7 convert_bitcast_fusion.2
  840.7 5.3 fusion.89
  848.9 9.0 bitcast_add_fusion.4
  858.0 4.6 convert_bitcast_fusion.2
  867.4 5.3 fusion.89
  875.6 8.9 bitcast_add_fusion.4
  884.6 5.3 copy.35
  899.9 40.2 %psum.7 = f32[8192]{0:T(1024)} all-reduce(f32[8192]{0:T(1024)S(1)} %get-tuple-element.743), channel_id=1, replica_groups=mesh['dp'=8,'tensor'=4] {'dp','tensor'}, use_global_device_ids=true, to_apply=%region_13.14 | all-reduce | flops 8192 | bytes 65536 | tf_op jit(solution)/shard_map/psum | solution.py:131
  940.1 4.6 fusion.43
  (233 shorter events, 335.1 us)
Async XLA Ops:
  7.2 6.4 copy-start
  7.2 158.2 %all-gather.6.cloned.1.call-start = ((), (), s32[]{:S(2)}) async-start(), calls=%async_computation.3 | async-start | bytes 10485760 | tf_op jit(solution)/shard_map/all_gather | solution.py:63
  9.3 9.5 %copy-start.2 = (f32[128]{0:T(128)}, f32[128]{0:T(128)S(1)}, u32[]{:S(2)}) copy-start(f32[128]{0:T(128)S(1)} %add_rsqrt_fusion) | copy-start | bytes 1540
  12.8 6.0 copy-start.5
  12.9 7.4 copy-start.4
  12.9 183.3 %all-gather.4.cloned.1.call-start = ((), (), s32[]{:S(2)}) async-start(), calls=%async_computation.2 | async-start | bytes 2949120 | tf_op jit(solution)/shard_map/all_gather | solution.py:74
  14.4 879.8 %reduce-scatter.5.cloned.1.call-start = ((), (), s32[]{:S(2)}) async-start(), calls=%async_computation.5 | async-start | bytes 2949120 | tf_op jit(solution)/shard_map/reduce_scatter | solution.py:125
  670.9 225.2 %reduce-scatter.3.cloned.1.call-start = ((), (), s32[]{:S(2)}) async-start(), calls=%async_computation.4 | async-start | bytes 10485760 | tf_op jit(solution)/shard_map/reduce_scatter | solution.py:122
  889.8 6.3 copy-start.1
  889.8 6.3 copy-start.3
Sparse Core Ops, SparseCore 0:
  13.0 152.3 all-gather.5
  167.8 28.3 all-gather.3
  671.1 43.6 reduce-scatter.4
  717.0 144.4 reduce-scatter.2
where the time goes:
time: 955 us; the launch traced here: 951 us
  matrix products  535 us (56%)
  local copies, waits for them, and re-layouts  159 us (17%)
  waiting for transfers between devices  158 us (17%)
  blocking collectives  49.7 us (5%)
  other arithmetic  33.7 us (4%)
  between operations  15.2 us (2%)
    dot_general x24, matrix products, place_tiles(): jnp.einsum('nsi,sr->nri', lower_half, chooser, preferred_element_type=jnp...  232 us
    all_gather x1, waiting for transfers between devices, body(): gathered = lax.all_gather(normed, 'tensor', axis=0, tiled=True)  136 us
    dot_general x24, matrix products, place_tiles(): jnp.einsum('nsi,sr->nri', upper_half, chooser, preferred_element_type=jnp...  115 us
    dot_general x56, matrix products, pick_tiles(): jnp.einsum('nri,sr->nsi', blocks, chooser, preferred_element_type=jnp.flo...  99.9 us
    convert_element_type x24, local copies, waits for them, and re-layouts, place_tiles(): upper_half = values.astype(jnp.bfloat16)  53.1 us
    psum x1, blocking collectives, body(): gain_grad = lax.psum(gain_part, ('dp', 'tensor'))  40.2 us
    convert_element_type x24, local copies, waits for them, and re-layouts, place_tiles(): lower_half = (values - upper_half.astype(jnp.float32)).astype(jnp.bfloat16)  39.5 us
    dot_general x16, matrix products, tile_group(): jnp.einsum('nsi,nsj->sij', picked_x, picked_g, preferred_element_type=jnp...  38.1 us
  transfers between devices with their start and end apart: 4, of which 2 were waited for; matrix products, arithmetic and copies ran while one was open for 25% of the time, Pallas kernels for 0%

commit v1 on v0

v1 whole, which is shorter than its diff:
```python
import functools

import jax
import jax.numpy as jnp
from jax import lax
from jax.experimental import pallas as pl
from jax.experimental.pallas import tpu as pltpu
from jax.sharding import PartitionSpec as P

EPSILON = 1e-05
VMEM_BYTES = 56 * 1024 * 1024


def lanes(block, tile):
    return pl.ds(pl.multiple_of(block * tile, tile), tile)


def project_kernel(ids_ref, x_ref, w_ref, out_ref, acc_ref, *, cols):
    owners, _, slots, tile, _ = w_ref.shape
    t = pl.program_id(0)
    acc_ref[...] = jnp.zeros_like(acc_ref)

    def owner_step(owner, carry):
        parts = []
        for s in range(slots):
            block = ids_ref[owner, t, s]
            left = x_ref[:, lanes(block // cols, tile)]
            parts.append(jnp.dot(left, w_ref[owner, 0, s], preferred_element_type=jnp.float32))
        for s in range(slots):
            place = lanes(ids_ref[owner, t, s] % cols, tile)
            acc_ref[:, place] += parts[s]
        return carry

    lax.fori_loop(0, owners, owner_step, 0)
    out_ref[0] = acc_ref[...].astype(out_ref.dtype)


def gradient_kernel(
    ids_ref, xt_ref, w_ref, g_ref, h_ref, inv_ref, gain_ref,
    tiles_ref, hgrad_ref, gpart_ref, acc_ref, *, cols,
):
    owners, _, slots, tile, _ = w_ref.shape
    tokens, width = acc_ref.shape
    t = pl.program_id(0)

    @pl.when(t == 0)
    def _():
        acc_ref[...] = jnp.zeros_like(acc_ref)

    def owner_step(owner, carry):
        parts = []
        for s in range(slots):
            block = ids_ref[owner, t, s]
            g = g_ref[0, :, lanes(block % cols, tile)]
            parts.append(
                lax.dot_general(
                    g, w_ref[owner, 0, s], (((1,), (1,)), ((), ())),
                    preferred_element_type=jnp.float32,
                )
            )
            left = xt_ref[lanes(block // cols, tile), :]
            tiles_ref[owner, 0, s] = jnp.dot(left, g, preferred_element_type=jnp.float32).astype(
                tiles_ref.dtype
            )
        for s in range(slots):
            place = lanes(ids_ref[owner, t, s] // cols, tile)
            acc_ref[:, place] += parts[s]
        return carry

    lax.fori_loop(0, owners, owner_step, 0)

    @pl.when(t == pl.num_programs(0) - 1)
    def _():
        rows = 16
        gpart_ref[...] = jnp.zeros_like(gpart_ref)

        def row_step(i, carry):
            at = pl.ds(pl.multiple_of(i * rows, rows), rows)
            inverse = inv_ref[at, :]
            unit = h_ref[at, :].astype(jnp.float32) * inverse
            row_grad = acc_ref[at, :]
            product = row_grad * unit
            gpart_ref[...] += jnp.sum(product, axis=0, keepdims=True)
            mean = jnp.mean(product * gain_ref[...], axis=-1, keepdims=True)
            hgrad_ref[at, :] = (
                inverse * (row_grad * gain_ref[...] - unit * mean)
            ).astype(hgrad_ref.dtype)
            return carry

        lax.fori_loop(0, tokens // rows, row_step, 0)


def body(hidden, norm_gain, tile_values, tile_ids, tile_counts, proj_grad):
    tokens, width = hidden.shape
    _, slots, tile, _ = tile_values.shape
    seq, part_cols = proj_grad.shape
    cols = part_cols // tile
    n_tensor = lax.axis_size("tensor")
    n_dp = lax.axis_size("dp")
    live = jnp.arange(slots) < tile_counts[0, 0]
    masked = jnp.where(live[:, None, None], tile_values[0], 0)

    ids = lax.all_gather(tile_ids[0], ("dp", "tensor"), axis=0, tiled=False)
    ids = ids.reshape(n_dp, n_tensor, slots)
    line = lax.all_gather(masked, "tensor", axis=0, tiled=False)
    weights = lax.all_gather(line, "dp", axis=0, tiled=False)
    grads = lax.all_to_all(
        proj_grad.reshape(n_tensor, tokens, part_cols), "tensor", split_axis=0, concat_axis=0
    )

    hidden_f = hidden.astype(jnp.float32)
    inverse = lax.rsqrt(jnp.mean(hidden_f * hidden_f, axis=-1, keepdims=True) + EPSILON)
    normed = (hidden_f * inverse * norm_gain).astype(jnp.bfloat16)
    flipped = normed.T

    whole = lambda *shape: pl.BlockSpec(shape, lambda t, ids: (0,) * len(shape))
    w_spec = pl.BlockSpec((n_dp, 1, slots, tile, tile), lambda t, ids: (0, t, 0, 0, 0))
    c_spec = pl.BlockSpec((1, tokens, part_cols), lambda t, ids: (t, 0, 0))
    total = n_dp * n_tensor * slots
    flops = 2 * total * tokens * tile * tile
    params = pltpu.CompilerParams(
        dimension_semantics=("arbitrary",), vmem_limit_bytes=VMEM_BYTES
    )
    projected = pl.pallas_call(
        functools.partial(project_kernel, cols=cols),
        out_shape=jax.ShapeDtypeStruct((n_tensor, tokens, part_cols), jnp.bfloat16),
        grid_spec=pltpu.PrefetchScalarGridSpec(
            num_scalar_prefetch=1,
            grid=(n_tensor,),
            in_specs=[whole(tokens, width), w_spec],
            out_specs=c_spec,
            scratch_shapes=[pltpu.VMEM((tokens, part_cols), jnp.float32)],
        ),
        compiler_params=params,
        cost_estimate=pl.CostEstimate(
            flops=4 * flops, bytes_accessed=2 * total * tile * tile, transcendentals=0
        ),
        name="project",
    )(ids, normed, weights)
    projections = lax.all_to_all(projected, "tensor", split_axis=0, concat_axis=0)
    projections = projections.reshape(seq, part_cols)

    tile_parts, hidden_grad, gain_part = pl.pallas_call(
        functools.partial(gradient_kernel, cols=cols),
        out_shape=(
            jax.ShapeDtypeStruct((n_dp, n_tensor, slots, tile, tile), jnp.bfloat16),
            jax.ShapeDtypeStruct((tokens, width), jnp.bfloat16),
            jax.ShapeDtypeStruct((1, width), jnp.float32),
        ),
        grid_spec=pltpu.PrefetchScalarGridSpec(
            num_scalar_prefetch=1,
            grid=(n_tensor,),
            in_specs=[
                whole(width, tokens), w_spec, c_spec, whole(tokens, width),
                whole(tokens, 1), whole(1, width),
            ],
            out_specs=[w_spec, whole(tokens, width), whole(1, width)],
            scratch_shapes=[pltpu.VMEM((tokens, width), jnp.float32)],
        ),
        compiler_params=params,
        cost_estimate=pl.CostEstimate(
            flops=8 * flops, bytes_accessed=4 * total * tile * tile, transcendentals=0
        ),
        name="gradient",
    )(ids, flipped, weights, grads, hidden, inverse, norm_gain[None, :])

    plane = lax.psum_scatter(tile_parts, "dp", scatter_dimension=0, tiled=False)
    tile_sum = lax.psum_scatter(plane, "tensor", scatter_dimension=0, tiled=False)
    tile_grads = jnp.where(live[:, None, None], tile_sum.astype(jnp.float32), 0.0)[None]
    gain_grad = lax.psum(gain_part[0], ("dp", "tensor"))
    return (projections, hidden_grad, tile_grads, gain_grad)


def solution(mesh):
    in_specs = (
        P(("dp", "tensor"), None),
        P(),
        P("tensor", "dp", None, None),
        P("tensor", "dp"),
        P("tensor", "dp"),
        P("dp", "tensor"),
    )
    out_specs = (P("dp", "tensor"), P(("dp", "tensor"), None), P("tensor", "dp", None, None), P())
    return jax.shard_map(body, mesh=mesh, in_specs=in_specs, out_specs=out_specs, check_vma=False)
```

time: 955 us -> 330 us (0.35)
  matrix products: 535 us -> 0 us
  local copies, waits for them, and re-layouts: 159 us -> 10.7 us
  blocking collectives: 49.7 us -> 155 us
  waiting for transfers between devices: 158 us -> 87.5 us
  Pallas kernels: 0 us -> 38.7 us
  other arithmetic: 33.7 us -> 13.4 us
    dot_general x144 -> x0, matrix products: 535 us -> none  [the longest x24 232 us: place_tiles(): jnp.einsum('nsi,sr->nri', lower_half, chooser, preferred_element_type=jnp...]
    all_gather x2, waiting for transfers between devices: 157 us -> 35.8 us  [the longest x1 35.8 us: body(): line = lax.all_gather(masked, 'tensor', axis=0, tiled=False)]
    all_gather x1, blocking collectives: 9.46 us -> 113 us  [body(): ids = lax.all_gather(tile_ids[0], ('dp', 'tensor'), axis=0, tiled=False)]
    convert_element_type x48 -> x1, local copies, waits for them, and re-layouts: 92.6 us -> 4.45 us  [body(): normed = (hidden_f * inverse * norm_gain).astype(jnp.bfloat16)]
    reduce_scatter x2, waiting for transfers between devices: 0.01 us -> 51.6 us  [the longest x1 51.6 us: body(): plane = lax.psum_scatter(tile_parts, 'dp', scatter_dimension=0, tiled=False)]
    pallas_call x0 -> x2, Pallas kernels: none -> 38.7 us  [the longest x1 24.2 us: body(): pl.pallas_call(functools.partial(gradient_kernel, cols=cols), out_shape=(...]
    dynamic_update_slice x2 -> x0, local copies, waits for them, and re-layouts: 20.1 us -> none  [row_block(): row_grad = lax.dynamic_update_slice_in_dim(row_grad, rounded, begin, 0)]
    convert_element_type x7 -> x1, other arithmetic: 21.6 us -> 4.3 us  [body(): normed = (hidden_f * inverse * norm_gain).astype(jnp.bfloat16)]
  transfers between devices with their start and end apart: 4 -> 6, of which waited for: 2 -> 2; matrix products, arithmetic and copies ran while one was open for 25% -> 6% of each run, Pallas kernels for 0% -> 4%
where the time goes in v1:
time: 330 us; the launch traced here: 329 us
  blocking collectives  155 us (47%)
  waiting for transfers between devices  87.5 us (27%)
  Pallas kernels  38.7 us (12%)
  between operations  14.5 us (4%)
  other arithmetic  13.4 us (4%)
  local copies, waits for them, and re-layouts  10.7 us (3%)
  starting transfers between devices  8.51 us (3%)
    all_gather x1, blocking collectives, body(): ids = lax.all_gather(tile_ids[0], ('dp', 'tensor'), axis=0, tiled=False)  113 us
    reduce_scatter x1, waiting for transfers between devices, body(): plane = lax.psum_scatter(tile_parts, 'dp', scatter_dimension=0, tiled=False)  51.6 us
    psum x1, blocking collectives, body(): gain_grad = lax.psum(gain_part[0], ('dp', 'tensor'))  42.5 us
    all_gather x1, waiting for transfers between devices, body(): line = lax.all_gather(masked, 'tensor', axis=0, tiled=False)  35.8 us
    pallas_call x1, Pallas kernels, body(): pl.pallas_call(functools.partial(gradient_kernel, cols=cols), out_shape=(...  24.2 us
    pallas_call x1, Pallas kernels, body(): pl.pallas_call(functools.partial(project_kernel, cols=cols), out_shape=ja...  14.5 us
  transfers between devices with their start and end apart: 6, of which 2 were waited for; matrix products, arithmetic and copies ran while one was open for 6% of the time, Pallas kernels for 4%

profile of v1, /device:TPU:0, one launch (start us, length us, event | category | flops | bytes accessed | tf_op | source)
XLA Modules:
  0.0 328.8 jit_solution(669276591378141092)
XLA Ops:
  7.2 0.0 all-gather.5.cloned.1.call-start
  7.9 1.8 broadcast_select_fusion
  9.7 0.0 all-gather.5.cloned.1.call-update
  9.7 0.0 all-gather.7.cloned.1.call-start
  9.7 35.8 %all-gather.5.cloned.1.call-done = bf16[4,10,128,128]{3,2,1,0:T(8,128)(2,1)} async-done(((bf16[1,10,128,128]{3,2,1,0:T(8,128)(2,1)}), bf16[4,10,128,128]{3,2,1,0:T(8,128)(2,1)}) %all-gather.5.cloned.1.call-update) | async-done | bytes 1310736 | tf_op jit(solution)/shard_map/all_gather | solution.py:105
  45.6 0.0 all-gather.7.cloned.1.call-update
  45.6 4.6 %all-to-all-start.1 = ((bf16[4,128,2560]{2,1,0:T(8,128)(2,1)}), bf16[4,128,2560]{2,1,0:T(8,128)(2,1)}, u32[]{:S(2)}, u32[]{:S(2)}) async-start(bf16[4,128,2560]{2,1,0:T(8,128)(2,1)} %bitcast.15), calls=%async_computation.1 | async-start | bytes 5242880 | tf_op jit(solution)/shard_map/all_to_all | solution.py:107
  50.2 0.0 copy-start.3
  50.2 0.0 copy-start
  50.2 0.0 reduce-scatter.3.cloned.1.call-start
  50.2 3.3 %copy.13 = bf16[128,8192]{0,1:T(8,128)(2,1)S(1)} copy(bf16[128,8192]{1,0:T(8,128)(2,1)} %h_ref.1) | data formatting | bytes 4194304 | tf_op args[0]
  53.6 1.1 fusion
  54.7 0.7 copy.15.inv_ref
  55.4 0.0 copy-done.3
  55.4 112.9 %all-gather.1 = s32[32,1,10]{2,1,0:T(1,128)} all-gather(s32[1,1,10]{2,1,0:T(1,128)S(1)} %bitcast.21), channel_id=1, replica_groups=mesh['dp'=8,'tensor'=4] {'dp','tensor'}, dimensions={0}, use_global_device_ids=true | all-gather | bytes 1320 | tf_op jit(solution)/shard_map/all_gather | solution.py:103
  168.3 0.0 copy-done
  168.3 4.3 %fusion.4.xt_ref = bf16[8192,128]{1,0:T(8,128)(2,1)} fusion(f32[8192]{0:T(1024)S(1)} %copy-done, f32[128]{0:T(128)S(1)} %get-tuple-element.11, bf16[128,8192]{0,1:T(8,128)(2,1)S(1)} %copy.13), kind=kLoop, calls=%fused_computation.10 | loop fusion | flops 4194304 | bytes 4227584 | tf_op jit(solution)/shard_map/transpose | solution.py:114
  172.6 0.0 all-to-all-done.1.g_ref
  172.6 0.0 all-gather.7.cloned.1.call-done
  172.6 24.2 %gradient.1 = (bf16[8,4,10,128,128]{4,3,2,1,0:T(8,128)(2,1)}, bf16[128,8192]{1,0:T(8,128)(2,1)}, f32[1,8192]{1,0:T(1,128)}) custom-call(s32[8,4,10]{2,1,0:T(4,128)} %bitcast.19, bf16[8192,128]{1,0:T(8,128)(2,1)} %fusion.4.xt_ref, bf16[8,4,10,128,128]{4,3,2,1,0:T(8,128)(2,1)} %bitcast.22, bf16[4,128,2560]{2,1,0:T(8,128)(2,1)} %all-to-all-done.1.g_ref, ...), custom_call_target="tpu_custom_call" | custom-call | flops 10737418240 | bytes 20971520 | tf_op jit(solution)/shard_map/gradient/pallas_call | solution.py:143
  196.8 0.0 copy-start.1
  196.9 0.0 reduce-scatter.3.cloned.1.call-update
  196.9 0.7 copy-done.1
  197.6 4.3 %fusion.2 = bf16[128,8192]{0,1:T(8,128)(2,1)} fusion(bf16[128,8192]{0,1:T(8,128)(2,1)S(1)} %copy.13, f32[8192]{0:T(1024)S(1)} %copy-done.1, f32[128]{0:T(128)S(1)} %get-tuple-element.11), kind=kLoop, calls=%fused_computation.4 | loop fusion | flops 4194304 | bytes 4227584 | tf_op jit(solution)/shard_map/convert_element_type | solution.py:113
  201.9 4.5 %copy.14.x_ref = bf16[128,8192]{1,0:T(8,128)(2,1)} copy(bf16[128,8192]{0,1:T(8,128)(2,1)} %fusion.2) | data formatting | bytes 4194304 | tf_op jit(solution)/shard_map/convert_element_type | solution.py:113
  206.4 14.5 %project.1 = bf16[4,128,2560]{2,1,0:T(8,128)(2,1)} custom-call(s32[8,4,10]{2,1,0:T(4,128)} %bitcast.20, bf16[128,8192]{1,0:T(8,128)(2,1)} %copy.14.x_ref, bf16[8,4,10,128,128]{4,3,2,1,0:T(8,128)(2,1)} %bitcast.23), custom_call_target="tpu_custom_call" | custom-call | flops 5368709120 | bytes 10485760 | tf_op jit(solution)/shard_map/project/pallas_call | solution.py:124
  220.8 0.0 copy-start.2
  220.8 3.8 %all-to-all-start = ((bf16[4,128,2560]{2,1,0:T(8,128)(2,1)}), bf16[4,128,2560]{2,1,0:T(8,128)(2,1)S(1)}, u32[]{:S(2)}, u32[]{:S(2)}) async-start(bf16[4,128,2560]{2,1,0:T(8,128)(2,1)} %project.1), calls=%async_computation | async-start | bytes 5242880 | tf_op jit(solution)/shard_map/all_to_all | solution.py:140
  224.6 0.0 reduce-scatter.5.cloned.1.call-start
  224.7 51.6 %reduce-scatter.3.cloned.1.call-done = bf16[1,4,10,128,128]{4,3,2,1,0:T(8,128)(2,1)} async-done(((bf16[8,4,10,128,128]{4,3,2,1,0:T(8,128)(2,1)}), bf16[1,4,10,128,128]{4,3,2,1,0:T(8,128)(2,1)}) %reduce-scatter.3.cloned.1.call-update) | async-done | bytes 1310736 | tf_op jit(solution)/shard_map/reduce_scatter | solution.py:167
  276.3 0.0 reduce-scatter.5.cloned.1.call-update
  276.3 0.0 copy-done.2
  276.3 42.5 %psum.7 = f32[8192]{0:T(1024)} all-reduce(f32[8192]{0:T(1024)S(1)} %bitcast.18), channel_id=1, replica_groups=mesh['dp'=8,'tensor'=4] {'dp','tensor'}, use_global_device_ids=true, to_apply=%region_3.4 | all-reduce | flops 8192 | bytes 65536 | tf_op jit(solution)/shard_map/psum | solution.py:170
  318.9 0.0 all-to-all-done
  318.9 0.0 reduce-scatter.5.cloned.1.call-done
  318.9 1.9 convert_select_fusion
  320.8 1.5 copy.18
  (2 shorter events, 0.0 us)
Async XLA Ops:
  7.2 38.4 %all-gather.5.cloned.1.call-start = ((), (), s32[]{:S(2)}) async-start(), calls=%async_computation.4 | async-start | bytes 1638400 | tf_op jit(solution)/shard_map/all_gather | solution.py:105
  9.7 162.9 %all-gather.7.cloned.1.call-start = ((), (), s32[]{:S(2)}) async-start(), calls=%async_computation.7 | async-start | bytes 11796480 | tf_op jit(solution)/shard_map/all_gather | solution.py:106
  45.6 127.0 %all-to-all-start.1 = ((bf16[4,128,2560]{2,1,0:T(8,128)(2,1)}), bf16[4,128,2560]{2,1,0:T(8,128)(2,1)}, u32[]{:S(2)}, u32[]{:S(2)}) async-start(bf16[4,128,2560]{2,1,0:T(8,128)(2,1)} %bitcast.15), calls=%async_computation.1 | async-start | bytes 5242880 | tf_op jit(solution)/shard_map/all_to_all | solution.py:107
  50.2 5.2 %copy-start.3 = (s32[1,10]{1,0:T(1,128)S(1)}, s32[1,10]{1,0:T(1,128)}, u32[]{:S(2)}) copy-start(s32[1,10]{1,0:T(1,128)} %param.9) | copy-start | bytes 124
  50.2 118.1 %copy-start = (f32[8192]{0:T(1024)S(1)}, f32[8192]{0:T(1024)}, u32[]{:S(2)}) copy-start(f32[8192]{0:T(1024)} %param.7) | copy-start | bytes 98308
  50.2 226.1 %reduce-scatter.3.cloned.1.call-start = ((), (), s32[]{:S(2)}) async-start(), calls=%async_computation.5 | async-start | bytes 11796480 | tf_op jit(solution)/shard_map/reduce_scatter | solution.py:167
  196.8 0.8 copy-start.1
  220.8 55.5 %copy-start.2 = (f32[1,8192]{1,0:T(1,128)S(1)}, f32[1,8192]{1,0:T(1,128)}, u32[]{:S(2)}) copy-start(f32[1,8192]{1,0:T(1,128)} %get-tuple-element.9) | copy-start | bytes 98308
  220.8 98.0 %all-to-all-start = ((bf16[4,128,2560]{2,1,0:T(8,128)(2,1)}), bf16[4,128,2560]{2,1,0:T(8,128)(2,1)S(1)}, u32[]{:S(2)}, u32[]{:S(2)}) async-start(bf16[4,128,2560]{2,1,0:T(8,128)(2,1)} %project.1), calls=%async_computation | async-start | bytes 5242880 | tf_op jit(solution)/shard_map/all_to_all | solution.py:140
  224.6 94.2 %reduce-scatter.5.cloned.1.call-start = ((), (), s32[]{:S(2)}) async-start(), calls=%async_computation.6 | async-start | bytes 1638400 | tf_op jit(solution)/shard_map/reduce_scatter | solution.py:168
Sparse Core Ops, SparseCore 0:
  10.1 35.3 all-gather.4
  47.5 62.2 all-gather.6
  197.0 79.2 reduce-scatter.2
  278.4 32.1 reduce-scatter.4

commit v2 on v1

--- a/solution.py
+++ b/solution.py
@@ -9,14 +9,305 @@
 
 EPSILON = 1e-05
 VMEM_BYTES = 56 * 1024 * 1024
+MESH = pl.DeviceIdType.MESH
+TAIL = 16
 
 
 def lanes(block, tile):
     return pl.ds(pl.multiple_of(block * tile, tile), tile)
 
 
+def spread_kernel(
+    tiles_ref, g_ref, h_ref, gain_ref,
+    w_ref, grads_ref, x_ref, xt_ref, inv_ref,
+    z_send, z_recv, p_send, p_recv, c_send, c_recv, a_send, a_recv, l_sem,
+    *, pairs, n_tensor, tile,
+):
+    d = lax.axis_index("dp")
+    t = lax.axis_index("tensor")
+    core = lax.rem(d, 2)
+    pair = d // 2
+    other = pair * 2 + 1 - core
+
+    def line(k):
+        return lax.rem(t + k + n_tensor, n_tensor)
+
+    def peer(j):
+        return lax.rem(pair + j + pairs, pairs) * 2 + core
+
+    greet(d, t, other, peer, line, pairs, n_tensor)
+
+    def remote(src, dst, send, recv, to):
+        return pltpu.make_async_remote_copy(
+            src_ref=src, dst_ref=dst, send_sem=send, recv_sem=recv,
+            device_id=to, device_id_type=MESH,
+        )
+
+    def over_line(k):
+        return remote(
+            tiles_ref, w_ref.at[d, t], z_send.at[k], z_recv.at[k], (d, line(k))
+        )
+
+    def over_plane(k, j):
+        slot = w_ref.at[d, line(-k)]
+        src = tiles_ref if k == 0 else slot
+        return remote(src, slot, p_send.at[k, j], p_recv.at[k, j], (peer(j), t))
+
+    def over_core(k, j):
+        slot = w_ref.at[peer(-j), line(-k)]
+        src = tiles_ref if k == 0 and j == 0 else slot
+        return remote(src, slot, c_send.at[k, j], c_recv.at[k, j], (other, t))
+
+    def exchange(k):
+        return remote(
+            g_ref.at[line(k)], grads_ref.at[t], a_send.at[k], a_recv.at[k], (d, line(k))
+        )
+
+    def landed(slot, send, recv):
+        remote(slot, slot, send, recv, (other, t)).wait_recv()
+
+    for k in range(1, n_tensor):
+        over_line(k).start()
+    for j in range(1, pairs):
+        over_plane(0, j).start()
+    over_core(0, 0).start()
+    own = (
+        pltpu.make_async_copy(tiles_ref, w_ref.at[d, t], l_sem.at[0]),
+        pltpu.make_async_copy(g_ref.at[t], grads_ref.at[t], l_sem.at[1]),
+    )
+    for copy in own:
+        copy.start()
+
+    tokens, width = h_ref.shape
+    rows = 16
+
+    def norm_step(i, carry):
+        at = pl.ds(pl.multiple_of(i * rows, rows), rows)
+        hidden = h_ref[at, :].astype(jnp.float32)
+        inverse = lax.rsqrt(jnp.mean(hidden * hidden, axis=-1, keepdims=True) + EPSILON)
+        inv_ref[at, :] = inverse
+        x_ref[at, :] = (hidden * inverse * gain_ref[...]).astype(x_ref.dtype)
+        return carry
+
+    lax.fori_loop(0, tokens // rows, norm_step, 0)
+
+    for k in range(1, n_tensor):
+        landed(w_ref.at[d, line(-k)], z_send.at[k], z_recv.at[k])
+        for j in range(1, pairs):
+            over_plane(k, j).start()
+        over_core(k, 0).start()
+    for k in range(1, n_tensor):
+        exchange(k).start()
+
+    def flip_step(i, carry):
+        at = lanes(i, tile)
+        xt_ref[at, :] = x_ref[:, at].astype(jnp.float32).T.astype(xt_ref.dtype)
+        return carry
+
+    lax.fori_loop(0, width // tile, flip_step, 0)
+
+    for k in range(n_tensor):
+        for j in range(1, pairs):
+            landed(w_ref.at[peer(-j), line(-k)], p_send.at[k, j], p_recv.at[k, j])
+            over_core(k, j).start()
+    for k in range(n_tensor):
+        for j in range(pairs):
+            far = lax.rem(pair - j + pairs, pairs) * 2 + 1 - core
+            landed(w_ref.at[far, line(-k)], c_send.at[k, j], c_recv.at[k, j])
+    for k in range(1, n_tensor):
+        landed(grads_ref.at[line(-k)], a_send.at[k], a_recv.at[k])
+    for copy in own:
+        copy.wait()
+    for k in range(n_tensor):
+        if k:
+            over_line(k).wait_send()
+            exchange(k).wait_send()
+        for j in range(pairs):
+            if j:
+                over_plane(k, j).wait_send()
+            over_core(k, j).wait_send()
+
+
+def greet(d, t, other, peer, line, pairs, n_tensor):
+    barrier = pltpu.get_barrier_semaphore()
+    targets = [(other, t)]
+    targets += [(peer(j), t) for j in range(1, pairs)]
+    targets += [(d, line(k)) for k in range(1, n_tensor)]
+    for target in targets:
+        pl.semaphore_signal(barrier, inc=1, device_id=target, device_id_type=MESH)
+    pl.semaphore_wait(barrier, len(targets))
+
+
+def collect_kernel(
+    parts_ref, out_in_ref, gain_ref, sum_ref, out_ref, total_ref,
+    mine, from_core, from_plane, from_line, g_core, g_plane, g_line,
+    c_send, c_recv, p_send, p_recv, z_send, z_recv, a_send, a_recv,
+    gc_send, gc_recv, gp_send, gp_recv, gz_send, gz_recv, l_sem, o_sem,
+    *, pairs, n_tensor, tile,
+):
+    d = lax.axis_index("dp")
+    t = lax.axis_index("tensor")
+    core = lax.rem(d, 2)
+    pair = d // 2
+    other = pair * 2 + 1 - core
+
+    def line(k):
+        return lax.rem(t + k + n_tensor, n_tensor)
+
+    def near(j):
+        return lax.rem(pair + j + pairs, pairs)
+
+    def peer(j):
+        return near(j) * 2 + core
+
+    greet(d, t, other, peer, line, pairs, n_tensor)
+
+    def remote(src, dst, send, recv, to):
+        return pltpu.make_async_remote_copy(
+            src_ref=src, dst_ref=dst, send_sem=send, recv_sem=recv,
+            device_id=to, device_id_type=MESH,
+        )
+
+    def over_core(j):
+        return remote(
+            parts_ref.at[near(j) * 2 + 1 - core], from_core.at[near(j)],
+            c_send.at[j], c_recv.at[j], (other, t),
+        )
+
+    def load_own(j):
+        return pltpu.make_async_copy(parts_ref.at[peer(j)], mine.at[near(j)], l_sem.at[j])
+
+    def over_plane(j, k):
+        return remote(
+            mine.at[near(j), line(k)], from_plane.at[pair, line(k)],
+            p_send.at[j, k], p_recv.at[j, k], (peer(j), t),
+        )
+
+    def over_line(k):
+        return remote(
+            mine.at[pair, line(k)], from_line.at[k], z_send.at[k], z_recv.at[k], (d, line(k))
+        )
+
+    def exchange(k):
+        return remote(
+            out_in_ref.at[line(k)], out_ref.at[t], a_send.at[k], a_recv.at[k], (d, line(k))
+        )
+
+    def landed(slot, send, recv):
+        remote(slot, slot, send, recv, (other, t)).wait_recv()
+
+    order = list(range(1, pairs)) + [0]
+    gain_core = remote(gain_ref, g_core, gc_send, gc_recv, (other, t))
+    gain_core.start()
+    for j in order:
+        over_core(j).start()
+        load_own(j).start()
+    for k in range(1, n_tensor):
+        exchange(k).start()
+    own_out = pltpu.make_async_copy(out_in_ref.at[t], out_ref.at[t], o_sem)
+    own_out.start()
+
+    gain_core.wait_recv()
+    g_plane[pair] = gain_ref[...] + g_core[...]
+    gain_plane = [
+        remote(g_plane.at[pair], g_plane.at[pair], gp_send.at[j], gp_recv.at[j], (peer(j), t))
+        for j in range(1, pairs)
+    ]
+    for copy in gain_plane:
+        copy.start()
+
+    steps = mine.shape[2] // tile
+    f32 = jnp.float32
+    lines = list(range(1, n_tensor)) + [0]
+    for j in range(1, pairs):
+        load_own(j).wait()
+        landed(from_core.at[near(j)], c_send.at[j], c_recv.at[j])
+        for k in lines:
+
+            def core_step(i, carry, j=j, k=k):
+                at = lanes(i, tile)
+                both = mine[near(j), line(k), at, :].astype(f32)
+                both += from_core[near(j), line(k), at, :].astype(f32)
+                mine[near(j), line(k), at, :] = both.astype(mine.dtype)
+                return carry
+
+            lax.fori_loop(0, steps, core_step, 0)
+            over_plane(j, k).start()
+    load_own(0).wait()
+    landed(from_core.at[pair], c_send.at[0], c_recv.at[0])
+
+    for j in range(1, pairs):
+        landed(g_plane.at[near(-j)], gp_send.at[j], gp_recv.at[j])
+    whole_plane = g_plane[0]
+    for p in range(1, pairs):
+        whole_plane += g_plane[p]
+    g_line[t] = whole_plane
+    gain_line = [
+        remote(g_line.at[t], g_line.at[t], gz_send.at[k], gz_recv.at[k], (d, line(k)))
+        for k in range(1, n_tensor)
+    ]
+    for copy in gain_line:
+        copy.start()
+
+    for k in lines:
+        for j in range(1, pairs):
+            landed(from_plane.at[near(-j), line(k)], p_send.at[j, k], p_recv.at[j, k])
+
+        def plane_step(i, carry, k=k):
+            at = lanes(i, tile)
+            total = mine[pair, line(k), at, :].astype(f32)
+            total += from_core[pair, line(k), at, :].astype(f32)
+            for j in range(1, pairs):
+                total += from_plane[near(-j), line(k), at, :].astype(f32)
+            if k:
+                mine[pair, line(k), at, :] = total.astype(mine.dtype)
+            else:
+                sum_ref[at, :] = total
+            return carry
+
+        lax.fori_loop(0, steps, plane_step, 0)
+        if k:
+            over_line(k).start()
+
+    for k in range(1, n_tensor):
+        landed(g_line.at[line(-k)], gz_send.at[k], gz_recv.at[k])
+    whole_line = g_line[0]
+    for q in range(1, n_tensor):
+        whole_line += g_line[q]
+    total_ref[...] = whole_line
+
+    for k in range(1, n_tensor):
+        landed(from_line.at[k], z_send.at[k], z_recv.at[k])
+
+    def line_step(i, carry):
+        at = lanes(i, tile)
+        total = sum_ref[at, :]
+        for k in range(1, n_tensor):
+            total += from_line[k, at, :].astype(f32)
+        sum_ref[at, :] = total
+        return carry
+
+    lax.fori_loop(0, steps, line_step, 0)
+
+    for k in range(1, n_tensor):
+        landed(out_ref.at[line(-k)], a_send.at[k], a_recv.at[k])
+    own_out.wait()
+    gain_core.wait_send()
+    for copy in gain_plane + gain_line:
+        copy.wait_send()
+    for j in range(pairs):
+        over_core(j).wait_send()
+        if j:
+            for k in range(n_tensor):
+                over_plane(j, k).wait_send()
+    for k in range(1, n_tensor):
+        over_line(k).wait_send()
+        exchange(k).wait_send()
+
+
 def project_kernel(ids_ref, x_ref, w_ref, out_ref, acc_ref, *, cols):
-    owners, _, slots, tile, _ = w_ref.shape
+    owners, slots = ids_ref.shape[0], ids_ref.shape[2]
+    tile = w_ref.shape[-1]
     t = pl.program_id(0)
     acc_ref[...] = jnp.zeros_like(acc_ref)
 
@@ -25,7 +316,7 @@
         for s in range(slots):
             block = ids_ref[owner, t, s]
             left = x_ref[:, lanes(block // cols, tile)]
-            parts.append(jnp.dot(left, w_ref[owner, 0, s], preferred_element_type=jnp.float32))
+            parts.append(jnp.dot(left, w_ref[owner, 0, s * tile:(s + 1) * tile, :], preferred_element_type=jnp.float32))
         for s in range(slots):
             place = lanes(ids_ref[owner, t, s] % cols, tile)
             acc_ref[:, place] += parts[s]
@@ -39,7 +330,8 @@
     ids_ref, xt_ref, w_ref, g_ref, h_ref, inv_ref, gain_ref,
     tiles_ref, hgrad_ref, gpart_ref, acc_ref, *, cols,
 ):
-    owners, _, slots, tile, _ = w_ref.shape
+    owners, slots = ids_ref.shape[0], ids_ref.shape[2]
+    tile = w_ref.shape[-1]
     tokens, width = acc_ref.shape
     t = pl.program_id(0)
 
@@ -54,12 +346,12 @@
             g = g_ref[0, :, lanes(block % cols, tile)]
             parts.append(
                 lax.dot_general(
-                    g, w_ref[owner, 0, s], (((1,), (1,)), ((), ())),
+                    g, w_ref[owner, 0, s * tile:(s + 1) * tile, :], (((1,), (1,)), ((), ())),
                     preferred_element_type=jnp.float32,
                 )
             )
             left = xt_ref[lanes(block // cols, tile), :]
-            tiles_ref[owner, 0, s] = jnp.dot(left, g, preferred_element_type=jnp.float32).astype(
+            tiles_ref[owner, 0, s * tile:(s + 1) * tile, :] = jnp.dot(left, g, preferred_element_type=jnp.float32).astype(
                 tiles_ref.dtype
             )
         for s in range(slots):
@@ -100,21 +392,42 @@
     live = jnp.arange(slots) < tile_counts[0, 0]
     masked = jnp.where(live[:, None, None], tile_values[0], 0)
 
-    ids = lax.all_gather(tile_ids[0], ("dp", "tensor"), axis=0, tiled=False)
-    ids = ids.reshape(n_dp, n_tensor, slots)
-    line = lax.all_gather(masked, "tensor", axis=0, tiled=False)
-    weights = lax.all_gather(line, "dp", axis=0, tiled=False)
-    grads = lax.all_to_all(
-        proj_grad.reshape(n_tensor, tokens, part_cols), "tensor", split_axis=0, concat_axis=0
-    )
-
-    hidden_f = hidden.astype(jnp.float32)
-    inverse = lax.rsqrt(jnp.mean(hidden_f * hidden_f, axis=-1, keepdims=True) + EPSILON)
-    normed = (hidden_f * inverse * norm_gain).astype(jnp.bfloat16)
-    flipped = normed.T
+    pairs = n_dp // 2
+    rows = slots * tile
+    numbers = jnp.stack([tile_ids[0] // cols, tile_ids[0] % cols]).astype(jnp.bfloat16)
+    numbers = jnp.pad(numbers, ((0, TAIL - 2), (0, tile - slots)))
+    packed = jnp.concatenate([masked.reshape(rows, tile), numbers], axis=0)
+    dma = pltpu.SemaphoreType.DMA
+    in_hbm = pl.BlockSpec(memory_space=pl.ANY)
+    in_vmem = pl.BlockSpec(memory_space=pltpu.VMEM)
+    weights, grads, normed, flipped, inverse = pl.pallas_call(
+        functools.partial(spread_kernel, pairs=pairs, n_tensor=n_tensor, tile=tile),
+        out_shape=(
+            jax.ShapeDtypeStruct((n_dp, n_tensor, rows + TAIL, tile), jnp.bfloat16),
+            jax.ShapeDtypeStruct((n_tensor, tokens, part_cols), jnp.bfloat16),
+            jax.ShapeDtypeStruct((tokens, width), jnp.bfloat16),
+            jax.ShapeDtypeStruct((width, tokens), jnp.bfloat16),
+            jax.ShapeDtypeStruct((tokens, 1), jnp.float32),
+        ),
+        in_specs=[in_hbm, in_hbm, in_vmem, in_vmem],
+        out_specs=[in_hbm, in_hbm, in_vmem, in_vmem, in_vmem],
+        scratch_shapes=[
+            dma((n_tensor,)), dma((n_tensor,)),
+            dma((n_tensor, pairs)), dma((n_tensor, pairs)),
+            dma((n_tensor, pairs)), dma((n_tensor, pairs)),
+            dma((n_tensor,)), dma((n_tensor,)), dma((2,)),
+        ],
+        compiler_params=pltpu.CompilerParams(
+            collective_id=0, has_side_effects=True, vmem_limit_bytes=VMEM_BYTES
+        ),
+        name="spread",
+    )(packed, proj_grad.reshape(n_tensor, tokens, part_cols), hidden, norm_gain[None, :])
+    numbers = weights[:, :, rows:rows + 2, :slots].astype(jnp.int32)
+    ids = numbers[:, :, 0] * cols + numbers[:, :, 1]
 
     whole = lambda *shape: pl.BlockSpec(shape, lambda t, ids: (0,) * len(shape))
-    w_spec = pl.BlockSpec((n_dp, 1, slots, tile, tile), lambda t, ids: (0, t, 0, 0, 0))
+    w_spec = pl.BlockSpec((n_dp, 1, rows + TAIL, tile), lambda t, ids: (0, t, 0, 0))
+    t_spec = pl.BlockSpec((n_dp, 1, rows, tile), lambda t, ids: (0, t, 0, 0))
     c_spec = pl.BlockSpec((1, tokens, part_cols), lambda t, ids: (t, 0, 0))
     total = n_dp * n_tensor * slots
     flops = 2 * total * tokens * tile * tile
@@ -137,13 +450,10 @@
         ),
         name="project",
     )(ids, normed, weights)
-    projections = lax.all_to_all(projected, "tensor", split_axis=0, concat_axis=0)
-    projections = projections.reshape(seq, part_cols)
-
     tile_parts, hidden_grad, gain_part = pl.pallas_call(
         functools.partial(gradient_kernel, cols=cols),
         out_shape=(
-            jax.ShapeDtypeStruct((n_dp, n_tensor, slots, tile, tile), jnp.bfloat16),
+            jax.ShapeDtypeStruct((n_dp, n_tensor, rows, tile), jnp.bfloat16),
             jax.ShapeDtypeStruct((tokens, width), jnp.bfloat16),
             jax.ShapeDtypeStruct((1, width), jnp.float32),
         ),
@@ -154,7 +464,7 @@
                 whole(width, tokens), w_spec, c_spec, whole(tokens, width),
                 whole(tokens, 1), whole(1, width),
             ],
-            out_specs=[w_spec, whole(tokens, width), whole(1, width)],
+            out_specs=[t_spec, whole(tokens, width), whole(1, width)],
             scratch_shapes=[pltpu.VMEM((tokens, width), jnp.float32)],
         ),
         compiler_params=params,
@@ -164,10 +474,48 @@
         name="gradient",
     )(ids, flipped, weights, grads, hidden, inverse, norm_gain[None, :])
 
-    plane = lax.psum_scatter(tile_parts, "dp", scatter_dimension=0, tiled=False)
-    tile_sum = lax.psum_scatter(plane, "tensor", scatter_dimension=0, tiled=False)
-    tile_grads = jnp.where(live[:, None, None], tile_sum.astype(jnp.float32), 0.0)[None]
-    gain_grad = lax.psum(gain_part[0], ("dp", "tensor"))
+    chunk = (n_tensor, rows, tile)
+    held = 2 * (3 * pairs + 1) * n_tensor * rows * tile
+    if held < VMEM_BYTES // 2:
+        small = (8, width // 8)
+        f32 = jnp.float32
+        tile_sum, projections, gain_grad = pl.pallas_call(
+            functools.partial(collect_kernel, pairs=pairs, n_tensor=n_tensor, tile=tile),
+            out_shape=(
+                jax.ShapeDtypeStruct((rows, tile), f32),
+                jax.ShapeDtypeStruct((n_tensor, tokens, part_cols), jnp.bfloat16),
+                jax.ShapeDtypeStruct(small, f32),
+            ),
+            in_specs=[in_hbm, in_hbm, in_vmem],
+            out_specs=[in_vmem, in_hbm, in_vmem],
+            scratch_shapes=[
+                pltpu.VMEM((pairs,) + chunk, jnp.bfloat16),
+                pltpu.VMEM((pairs,) + chunk, jnp.bfloat16),
+                pltpu.VMEM((pairs,) + chunk, jnp.bfloat16),
+                pltpu.VMEM(chunk, jnp.bfloat16),
+                pltpu.VMEM(small, f32),
+                pltpu.VMEM((pairs,) + small, f32),
+                pltpu.VMEM((n_tensor,) + small, f32),
+                dma((pairs,)), dma((pairs,)),
+                dma((pairs, n_tensor)), dma((pairs, n_tensor)),
+                dma((n_tensor,)), dma((n_tensor,)), dma((n_tensor,)), dma((n_tensor,)),
+                dma, dma, dma((pairs,)), dma((pairs,)), dma((n_tensor,)), dma((n_tensor,)),
+                dma((pairs,)), dma,
+            ],
+            compiler_params=pltpu.CompilerParams(
+                collective_id=1, has_side_effects=True, vmem_limit_bytes=VMEM_BYTES
+            ),
+            name="collect",
+        )(tile_parts, projected, gain_part.reshape(small))
+        gain_grad = gain_grad.reshape(width)
+    else:
+        projections = lax.all_to_all(projected, "tensor", split_axis=0, concat_axis=0)
+        plane = lax.psum_scatter(tile_parts, "dp", scatter_dimension=0, tiled=False)
+        tile_sum = lax.psum_scatter(plane, "tensor", scatter_dimension=0, tiled=False)
+        gain_grad = lax.psum(gain_part[0], ("dp", "tensor"))
+    projections = projections.reshape(seq, part_cols)
+    tile_sum = tile_sum.reshape(slots, tile, tile).astype(jnp.float32)
+    tile_grads = jnp.where(live[:, None, None], tile_sum, 0.0)[None]
     return (projections, hidden_grad, tile_grads, gain_grad)
 
 

time: 330 us -> 265 us (0.80)
  Pallas kernels: 38.7 us -> 222 us
  blocking collectives: 155 us -> 0 us
  waiting for transfers between devices: 87.5 us -> 0 us
  local copies, waits for them, and re-layouts: 10.7 us -> 32.2 us
  between operations: 14.5 us -> 1.34 us
  starting transfers between devices: 8.51 us -> 0 us
  other arithmetic: 13.4 us -> 6.79 us
    pallas_call x0 -> x2, Pallas kernels: none -> 184 us  [the longest x1 100 us: body(): pl.pallas_call(functools.partial(collect_kernel, pairs=pairs, n_tensor=n_...]
    all_gather x1 -> x0, blocking collectives: 113 us -> none  [body(): ids = lax.all_gather(tile_ids[0], ('dp', 'tensor'), axis=0, tiled=False)]
    reduce_scatter x2 -> x0, waiting for transfers between devices: 51.6 us -> none  [the longest x1 51.6 us: body(): plane = lax.psum_scatter(tile_parts, 'dp', scatter_dimension=0, tiled=False)]
    psum x1 -> x0, blocking collectives: 42.5 us -> none  [body(): gain_grad = lax.psum(gain_part[0], ('dp', 'tensor'))]
    all_gather x2 -> x0, waiting for transfers between devices: 35.8 us -> none  [the longest x1 35.8 us: body(): line = lax.all_gather(masked, 'tensor', axis=0, tiled=False)]
    pallas_call x0 -> x2, local copies, waits for them, and re-layouts: none -> 26.8 us  [the longest x1 26.2 us: body(): pl.pallas_call(functools.partial(spread_kernel, pairs=pairs, n_tensor=n_t...]
    all_to_all x2 -> x0, starting transfers between devices: 8.35 us -> none  [the longest x1 4.56 us: body(): lax.all_to_all(proj_grad.reshape(n_tensor, tokens, part_cols), 'tensor',...]
    convert_element_type x1 -> x0, local copies, waits for them, and re-layouts: 4.45 us -> none  [body(): normed = (hidden_f * inverse * norm_gain).astype(jnp.bfloat16)]
  transfers between devices with their start and end apart: 6 -> 0, of which waited for: 2 -> 0; matrix products, arithmetic and copies ran while one was open for 6% -> 0% of each run, Pallas kernels for 4% -> 0%
where the time goes in v2:
time: 265 us; the launch traced here: 262 us
  Pallas kernels  222 us (84%)
  local copies, waits for them, and re-layouts  32.2 us (12%)
  other arithmetic  6.79 us (3%)
    pallas_call x1, Pallas kernels, body(): pl.pallas_call(functools.partial(collect_kernel, pairs=pairs, n_tensor=n_...  100 us
    pallas_call x1, Pallas kernels, body(): pl.pallas_call(functools.partial(spread_kernel, pairs=pairs, n_tensor=n_t...  83.4 us
    pallas_call x1, local copies, waits for them, and re-layouts, body(): pl.pallas_call(functools.partial(spread_kernel, pairs=pairs, n_tensor=n_t...  26.2 us
    pallas_call x1, Pallas kernels, body(): pl.pallas_call(functools.partial(gradient_kernel, cols=cols), out_shape=(...  24.2 us
    pallas_call x1, Pallas kernels, body(): pl.pallas_call(functools.partial(project_kernel, cols=cols), out_shape=ja...  13.4 us

profile of v2, /device:TPU:0, one launch (start us, length us, event | category | flops | bytes accessed | tf_op | source)
XLA Modules:
  0.0 261.9 jit_solution(4465015559260886210)
XLA Ops:
  0.6 0.7 fusion.8
  2.0 0.1 broadcast_bitcast_fusion
  2.1 1.2 bitcast_select_fusion
  3.3 0.7 pad_maximum_fusion.tiles_ref
  4.0 83.4 %spread.1 = (bf16[8,4,1296,128]{3,2,1,0:T(8,128)(2,1)}, bf16[4,128,2560]{2,1,0:T(8,128)(2,1)}, bf16[128,8192]{1,0:T(8,128)(2,1)}, bf16[8192,128]{1,0:T(8,128)(2,1)}, f32[128,1]{1,0:T(8,128)}) custom-call(bf16[1296,128]{1,0:T(8,128)(2,1)} %pad_maximum_fusion.tiles_ref, bf16[4,128,2560]{2,1,0:T(8,128)(2,1)} %bitcast.17, bf16[128,8192]{1,0:T(8,128)(2,1)} %h_ref.3, ...), custom_call_target="tpu_custom_call" | custom-call | tf_op jit(solution)/shard_map/spread/pallas_call | solution.py:403
  87.4 26.2 %copy.10 = bf16[8,4,1296,128]{3,1,0,2:T(4,128)(2,1)S(1)} copy(bf16[8,4,1296,128]{3,2,1,0:T(8,128)(2,1)} %get-tuple-element.15.w_ref) | data formatting | bytes 21233664 | tf_op jit(solution)/shard_map/spread/pallas_call | solution.py:403
  113.7 0.6 fusion.ids_ref
  114.3 24.2 %gradient.1 = (bf16[8,4,1280,128]{3,2,1,0:T(8,128)(2,1)}, bf16[128,8192]{1,0:T(8,128)(2,1)}, f32[1,8192]{1,0:T(1,128)}) custom-call(s32[8,4,10]{2,1,0:T(4,128)} %fusion.ids_ref, bf16[8192,128]{1,0:T(8,128)(2,1)} %get-tuple-element.16.xt_ref, bf16[8,4,1296,128]{3,2,1,0:T(8,128)(2,1)} %get-tuple-element.15.w_ref, ...), custom_call_target="tpu_custom_call" | custom-call | flops 10737418240 | bytes 20971520 | tf_op jit(solution)/shard_map/gradient/pallas_call | solution.py:453
  138.6 0.5 broadcast.55
  139.1 1.5 reduce.3
  140.6 0.6 reshape.44.gain_ref
  141.2 13.4 %project.1.out_in_ref = bf16[4,128,2560]{2,1,0:T(8,128)(2,1)} custom-call(s32[8,4,10]{2,1,0:T(4,128)} %fusion.ids_ref, bf16[128,8192]{1,0:T(8,128)(2,1)} %get-tuple-element.20.x_ref, bf16[8,4,1296,128]{3,2,1,0:T(8,128)(2,1)} %get-tuple-element.15.w_ref), custom_call_target="tpu_custom_call" | custom-call | flops 5368709120 | bytes 10485760 | tf_op jit(solution)/shard_map/project/pallas_call | solution.py:437
  154.6 100.4 %collect.1 = (f32[1280,128]{1,0:T(8,128)}, bf16[4,128,2560]{2,1,0:T(8,128)(2,1)}, f32[8,1024]{1,0:T(8,128)}) custom-call(bf16[8,4,1280,128]{3,2,1,0:T(8,128)(2,1)} %get-tuple-element.19.parts_ref, bf16[4,128,2560]{2,1,0:T(8,128)(2,1)} %project.1.out_in_ref, f32[8,1024]{1,0:T(8,128)} %reshape.44.gain_ref), custom_call_target="tpu_custom_call" | custom-call | tf_op jit(solution)/shard_map/collect/pallas_call | solution.py:482
  255.1 2.0 broadcast_select_fusion
  257.1 1.4 copy.13
  258.5 3.4 %copy.16 = bf16[512,2560]{1,0:T(8,128)(2,1)} copy(bf16[512,2560]{1,0:T(8,128)(2,1)} %bitcast.16) | data formatting | bytes 5242880
  (3 shorter events, 0.0 us)

commit v3 on v2

--- a/solution.py
+++ b/solution.py
@@ -19,8 +19,8 @@
 
 def spread_kernel(
     tiles_ref, g_ref, h_ref, gain_ref,
-    w_ref, grads_ref, x_ref, xt_ref, inv_ref,
-    z_send, z_recv, p_send, p_recv, c_send, c_recv, a_send, a_recv, l_sem,
+    w_ref, grads_ref, x_ref, xt_ref, inv_ref, tail_ref,
+    up_send, down_send, z_recv, p_send, p_recv, c_send, c_recv, a_send, a_recv, l_sem,
     *, pairs, n_tensor, tile,
 ):
     d = lax.axis_index("dp")
@@ -43,20 +43,16 @@
             device_id=to, device_id_type=MESH,
         )
 
-    def over_line(k):
-        return remote(
-            tiles_ref, w_ref.at[d, t], z_send.at[k], z_recv.at[k], (d, line(k))
-        )
-
-    def over_plane(k, j):
-        slot = w_ref.at[d, line(-k)]
-        src = tiles_ref if k == 0 else slot
-        return remote(src, slot, p_send.at[k, j], p_recv.at[k, j], (peer(j), t))
-
-    def over_core(k, j):
-        slot = w_ref.at[peer(-j), line(-k)]
-        src = tiles_ref if k == 0 and j == 0 else slot
-        return remote(src, slot, c_send.at[k, j], c_recv.at[k, j], (other, t))
+    def hop(q, step, src):
+        send = up_send if step > 0 else down_send
+        return remote(src, w_ref.at[d, q], send.at[q], z_recv.at[q], (d, t + step))
+
+    def over_plane(q, j, src):
+        return remote(src, w_ref.at[d, q], p_send.at[q, j], p_recv.at[q, j], (peer(j), t))
+
+    def over_core(q, j, src):
+        slot = w_ref.at[peer(-j), q]
+        return remote(src, slot, c_send.at[q, j], c_recv.at[q, j], (other, t))
 
     def exchange(k):
         return remote(
@@ -66,11 +62,20 @@
     def landed(slot, send, recv):
         remote(slot, slot, send, recv, (other, t)).wait_recv()
 
-    for k in range(1, n_tensor):
-        over_line(k).start()
-    for j in range(1, pairs):
-        over_plane(0, j).start()
-    over_core(0, 0).start()
+    def share(q, src):
+        for j in range(1, pairs):
+            over_plane(q, j, src).start()
+        over_core(q, 0, src).start()
+
+    @pl.when(t + 1 < n_tensor)
+    def _():
+        hop(t, 1, tiles_ref).start()
+
+    @pl.when(t > 0)
+    def _():
+        hop(t, -1, tiles_ref).start()
+
+    share(t, tiles_ref)
     own = (
         pltpu.make_async_copy(tiles_ref, w_ref.at[d, t], l_sem.at[0]),
         pltpu.make_async_copy(g_ref.at[t], grads_ref.at[t], l_sem.at[1]),
@@ -91,11 +96,23 @@
 
     lax.fori_loop(0, tokens // rows, norm_step, 0)
 
-    for k in range(1, n_tensor):
-        landed(w_ref.at[d, line(-k)], z_send.at[k], z_recv.at[k])
-        for j in range(1, pairs):
-            over_plane(k, j).start()
-        over_core(k, 0).start()
+    for far in range(1, n_tensor):
+        for step in (1, -1):
+            q = t - step * far
+            ends = (q >= 0) if step > 0 else (q < n_tensor)
+            more = (t + 1 < n_tensor) if step > 0 else (t > 0)
+
+            @pl.when(ends)
+            def _(q=q, step=step, more=more):
+                slot = w_ref.at[d, q]
+                landed(slot, p_send.at[q, 0], z_recv.at[q])
+
+                @pl.when(more)
+                def _():
+                    hop(q, step, slot).start()
+
+                share(q, slot)
+
     for k in range(1, n_tensor):
         exchange(k).start()
 
@@ -107,25 +124,41 @@
     lax.fori_loop(0, width // tile, flip_step, 0)
 
     for k in range(n_tensor):
+        q = line(-k)
         for j in range(1, pairs):
-            landed(w_ref.at[peer(-j), line(-k)], p_send.at[k, j], p_recv.at[k, j])
-            over_core(k, j).start()
+            slot = w_ref.at[peer(-j), q]
+            landed(slot, p_send.at[q, j], p_recv.at[q, j])
+            over_core(q, j, slot).start()
     for k in range(n_tensor):
+        q = line(-k)
         for j in range(pairs):
             far = lax.rem(pair - j + pairs, pairs) * 2 + 1 - core
-            landed(w_ref.at[far, line(-k)], c_send.at[k, j], c_recv.at[k, j])
+            landed(w_ref.at[far, q], c_send.at[q, j], c_recv.at[q, j])
+    for copy in own:
+        copy.wait()
+    tails = pltpu.make_async_copy(
+        w_ref.at[:, :, pl.ds(w_ref.shape[2] - TAIL, TAIL), :], tail_ref, l_sem.at[2]
+    )
+    tails.start()
     for k in range(1, n_tensor):
         landed(grads_ref.at[line(-k)], a_send.at[k], a_recv.at[k])
-    for copy in own:
-        copy.wait()
-    for k in range(n_tensor):
-        if k:
-            over_line(k).wait_send()
-            exchange(k).wait_send()
+    tails.wait()
+    for q in range(n_tensor):
+
+        @pl.when((q <= t) & (t + 1 < n_tensor))
+        def _(q=q):
+            hop(q, 1, w_ref.at[d, q]).wait_send()
+
+        @pl.when((q >= t) & (t > 0))
+        def _(q=q):
+            hop(q, -1, w_ref.at[d, q]).wait_send()
+
+        if q:
+            exchange(q).wait_send()
         for j in range(pairs):
             if j:
-                over_plane(k, j).wait_send()
-            over_core(k, j).wait_send()
+                over_plane(q, j, w_ref.at[d, q]).wait_send()
+            over_core(q, j, w_ref.at[peer(-j), q]).wait_send()
 
 
 def greet(d, t, other, peer, line, pairs, n_tensor):
@@ -139,10 +172,10 @@
 
 
 def collect_kernel(
-    parts_ref, out_in_ref, gain_ref, sum_ref, out_ref, total_ref,
+    parts_ref, gain_ref, sum_ref, total_ref,
     mine, from_core, from_plane, from_line, g_core, g_plane, g_line,
-    c_send, c_recv, p_send, p_recv, z_send, z_recv, a_send, a_recv,
-    gc_send, gc_recv, gp_send, gp_recv, gz_send, gz_recv, l_sem, o_sem,
+    c_send, c_recv, p_send, p_recv, z_send, z_recv,
+    gc_send, gc_recv, gp_send, gp_recv, gz_send, gz_recv, l_sem,
     *, pairs, n_tensor, tile,
 ):
     d = lax.axis_index("dp")
@@ -188,11 +221,6 @@
             mine.at[pair, line(k)], from_line.at[k], z_send.at[k], z_recv.at[k], (d, line(k))
         )
 
-    def exchange(k):
-        return remote(
-            out_in_ref.at[line(k)], out_ref.at[t], a_send.at[k], a_recv.at[k], (d, line(k))
-        )
-
     def landed(slot, send, recv):
         remote(slot, slot, send, recv, (other, t)).wait_recv()
 
@@ -202,10 +230,6 @@
     for j in order:
         over_core(j).start()
         load_own(j).start()
-    for k in range(1, n_tensor):
-        exchange(k).start()
-    own_out = pltpu.make_async_copy(out_in_ref.at[t], out_ref.at[t], o_sem)
-    own_out.start()
 
     gain_core.wait_recv()
     g_plane[pair] = gain_ref[...] + g_core[...]
@@ -289,9 +313,6 @@
 
     lax.fori_loop(0, steps, line_step, 0)
 
-    for k in range(1, n_tensor):
-        landed(out_ref.at[line(-k)], a_send.at[k], a_recv.at[k])
-    own_out.wait()
     gain_core.wait_send()
     for copy in gain_plane + gain_line:
         copy.wait_send()
@@ -302,7 +323,6 @@
                 over_plane(j, k).wait_send()
     for k in range(1, n_tensor):
         over_line(k).wait_send()
-        exchange(k).wait_send()
 
 
 def project_kernel(ids_ref, x_ref, w_ref, out_ref, acc_ref, *, cols):
@@ -400,7 +420,7 @@
     dma = pltpu.SemaphoreType.DMA
     in_hbm = pl.BlockSpec(memory_space=pl.ANY)
     in_vmem = pl.BlockSpec(memory_space=pltpu.VMEM)
-    weights, grads, normed, flipped, inverse = pl.pallas_call(
+    weights, grads, normed, flipped, inverse, tails = pl.pallas_call(
         functools.partial(spread_kernel, pairs=pairs, n_tensor=n_tensor, tile=tile),
         out_shape=(
             jax.ShapeDtypeStruct((n_dp, n_tensor, rows + TAIL, tile), jnp.bfloat16),
@@ -408,21 +428,22 @@
             jax.ShapeDtypeStruct((tokens, width), jnp.bfloat16),
             jax.ShapeDtypeStruct((width, tokens), jnp.bfloat16),
             jax.ShapeDtypeStruct((tokens, 1), jnp.float32),
+            jax.ShapeDtypeStruct((n_dp, n_tensor, TAIL, tile), jnp.bfloat16),
         ),
         in_specs=[in_hbm, in_hbm, in_vmem, in_vmem],
-        out_specs=[in_hbm, in_hbm, in_vmem, in_vmem, in_vmem],
+        out_specs=[in_hbm, in_hbm, in_vmem, in_vmem, in_vmem, in_vmem],
         scratch_shapes=[
-            dma((n_tensor,)), dma((n_tensor,)),
+            dma((n_tensor,)), dma((n_tensor,)), dma((n_tensor,)),
             dma((n_tensor, pairs)), dma((n_tensor, pairs)),
             dma((n_tensor, pairs)), dma((n_tensor, pairs)),
-            dma((n_tensor,)), dma((n_tensor,)), dma((2,)),
+            dma((n_tensor,)), dma((n_tensor,)), dma((3,)),
         ],
         compiler_params=pltpu.CompilerParams(
             collective_id=0, has_side_effects=True, vmem_limit_bytes=VMEM_BYTES
         ),
         name="spread",
     )(packed, proj_grad.reshape(n_tensor, tokens, part_cols), hidden, norm_gain[None, :])
-    numbers = weights[:, :, rows:rows + 2, :slots].astype(jnp.int32)
+    numbers = tails[:, :, :2, :slots].astype(jnp.int32)
     ids = numbers[:, :, 0] * cols + numbers[:, :, 1]
 
     whole = lambda *shape: pl.BlockSpec(shape, lambda t, ids: (0,) * len(shape))
@@ -450,6 +471,8 @@
         ),
         name="project",
     )(ids, normed, weights)
+    projected, grads = lax.optimization_barrier((projected, grads))
+    projections = lax.all_to_all(projected, "tensor", split_axis=0, concat_axis=0)
     tile_parts, hidden_grad, gain_part = pl.pallas_call(
         functools.partial(gradient_kernel, cols=cols),
         out_shape=(
@@ -479,15 +502,14 @@
     if held < VMEM_BYTES // 2:
         small = (8, width // 8)
         f32 = jnp.float32
-        tile_sum, projections, gain_grad = pl.pallas_call(
+        tile_sum, gain_grad = pl.pallas_call(
             functools.partial(collect_kernel, pairs=pairs, n_tensor=n_tensor, tile=tile),
             out_shape=(
                 jax.ShapeDtypeStruct((rows, tile), f32),
-                jax.ShapeDtypeStruct((n_tensor, tokens, part_cols), jnp.bfloat16),
                 jax.ShapeDtypeStruct(small, f32),
             ),
-            in_specs=[in_hbm, in_hbm, in_vmem],
-            out_specs=[in_vmem, in_hbm, in_vmem],
+            in_specs=[in_hbm, in_vmem],
+            out_specs=[in_vmem, in_vmem],
             scratch_shapes=[
                 pltpu.VMEM((pairs,) + chunk, jnp.bfloat16),
                 pltpu.VMEM((pairs,) + chunk, jnp.bfloat16),
@@ -498,18 +520,17 @@
                 pltpu.VMEM((n_tensor,) + small, f32),
                 dma((pairs,)), dma((pairs,)),
                 dma((pairs, n_tensor)), dma((pairs, n_tensor)),
-                dma((n_tensor,)), dma((n_tensor,)), dma((n_tensor,)), dma((n_tensor,)),
+                dma((n_tensor,)), dma((n_tensor,)),
                 dma, dma, dma((pairs,)), dma((pairs,)), dma((n_tensor,)), dma((n_tensor,)),
-                dma((pairs,)), dma,
+                dma((pairs,)),
             ],
             compiler_params=pltpu.CompilerParams(
                 collective_id=1, has_side_effects=True, vmem_limit_bytes=VMEM_BYTES
             ),
             name="collect",
-        )(tile_parts, projected, gain_part.reshape(small))
+        )(tile_parts, gain_part.reshape(small))
         gain_grad = gain_grad.reshape(width)
     else:
-        projections = lax.all_to_all(projected, "tensor", split_axis=0, concat_axis=0)
         plane = lax.psum_scatter(tile_parts, "dp", scatter_dimension=0, tiled=False)
         tile_sum = lax.psum_scatter(plane, "tensor", scatter_dimension=0, tiled=False)
         gain_grad = lax.psum(gain_part[0], ("dp", "tensor"))

time: 265 us -> 231 us (0.87); the launches traced: 262 us -> 231 us
  local copies, waits for them, and re-layouts: 32.2 us -> 5.04 us
  Pallas kernels: 222 us -> 212 us
  starting transfers between devices: 0 us -> 5.59 us
    pallas_call x1, local copies, waits for them, and re-layouts: 26.2 us -> 0.96 us  [body(): pl.pallas_call(functools.partial(spread_kernel, pairs=pairs, n_tensor=n_t...]
    pallas_call x1, Pallas kernels: 100 us -> 75.2 us  [body(): pl.pallas_call(functools.partial(collect_kernel, pairs=pairs, n_tensor=n_...]
    pallas_call x1, Pallas kernels: 83.4 us -> 99 us  [body(): pl.pallas_call(functools.partial(spread_kernel, pairs=pairs, n_tensor=n_t...]
    all_to_all x0 -> x1, starting transfers between devices: none -> 5.59 us  [body(): lax.all_to_all(projected, 'tensor', split_axis=0, concat_axis=0)]
  transfers between devices with their start and end apart: 0 -> 1, of which waited for: 0 -> 0; matrix products, arithmetic and copies ran while one was open for 0% -> 3% of each run, Pallas kernels for 0% -> 43%
where the time goes in v3:
time: 231 us
  Pallas kernels  212 us (92%)
  other arithmetic  6.78 us (3%)
  starting transfers between devices  5.59 us (2%)
  local copies, waits for them, and re-layouts  5.04 us (2%)
    pallas_call x1, Pallas kernels, body(): pl.pallas_call(functools.partial(spread_kernel, pairs=pairs, n_tensor=n_t...  99 us
    pallas_call x1, Pallas kernels, body(): pl.pallas_call(functools.partial(collect_kernel, pairs=pairs, n_tensor=n_...  75.2 us
    pallas_call x1, Pallas kernels, body(): pl.pallas_call(functools.partial(gradient_kernel, cols=cols), out_shape=(...  24.3 us
    pallas_call x1, Pallas kernels, body(): pl.pallas_call(functools.partial(project_kernel, cols=cols), out_shape=ja...  13.4 us
    all_to_all x1, starting transfers between devices, body(): lax.all_to_all(projected, 'tensor', split_axis=0, concat_axis=0)  5.59 us
  transfers between devices with their start and end apart: 1, of which 0 were waited for; matrix products, arithmetic and copies ran while one was open for 3% of the time, Pallas kernels for 43%

profile of v3, /device:TPU:0, one launch (start us, length us, event | category | flops | bytes accessed | tf_op | source)
XLA Modules:
  0.0 230.6 jit_solution(6551479339140960864)
XLA Ops:
  0.6 0.7 fusion.8
  2.0 0.1 broadcast_bitcast_fusion
  2.1 1.2 bitcast_select_fusion
  3.3 0.7 pad_maximum_fusion.tiles_ref
  4.0 99.0 %spread.1 = (bf16[8,4,1296,128]{3,2,1,0:T(8,128)(2,1)}, bf16[4,128,2560]{2,1,0:T(8,128)(2,1)}, bf16[128,8192]{1,0:T(8,128)(2,1)}, bf16[8192,128]{1,0:T(8,128)(2,...) custom-call(bf16[1296,128]{1,0:T(8,128)(2,1)} %pad_maximum_fusion.tiles_ref, bf16[4,128,2560]{2,1,0:T(8,128)(2,1)} %bitcast.17, ...), custom_call_target="tpu_custom_call" | custom-call | tf_op jit(solution)/shard_map/spread/pallas_call | solution.py:423
  103.0 1.0 copy.10
  104.0 0.6 fusion.ids_ref
  104.6 13.4 %project.1 = bf16[4,128,2560]{2,1,0:T(8,128)(2,1)} custom-call(s32[8,4,10]{2,1,0:T(4,128)} %fusion.ids_ref, bf16[128,8192]{1,0:T(8,128)(2,1)} %get-tuple-element.18.x_ref, bf16[8,4,1296,128]{3,2,1,0:T(8,128)(2,1)} %get-tuple-element.19.w_ref), custom_call_target="tpu_custom_call" | custom-call | flops 5368709120 | bytes 10485760 | tf_op jit(solution)/shard_map/project/pallas_call | solution.py:458
  118.0 5.6 %all-to-all-start = ((bf16[4,128,2560]{2,1,0:T(8,128)(2,1)}), bf16[4,128,2560]{2,1,0:T(8,128)(2,1)S(1)}, u32[]{:S(2)}, u32[]{:S(2)}) async-start(bf16[4,128,2560]{2,1,0:T(8,128)(2,1)} %project.1), calls=%async_computation | async-start | bytes 5242880 | tf_op jit(solution)/shard_map/all_to_all | solution.py:475
  123.6 24.3 %gradient.1 = (bf16[8,4,1280,128]{3,2,1,0:T(8,128)(2,1)}, bf16[128,8192]{1,0:T(8,128)(2,1)}, f32[1,8192]{1,0:T(1,128)}) custom-call(s32[8,4,10]{2,1,0:T(4,128)} %fusion.ids_ref, bf16[8192,128]{1,0:T(8,128)(2,1)} %get-tuple-element.22.xt_ref, bf16[8,4,1296,128]{3,2,1,0:T(8,128)(2,1)} %get-tuple-element.19.w_ref, ...), custom_call_target="tpu_custom_call" | custom-call | flops 10737418240 | bytes 20971520 | tf_op jit(solution)/shard_map/gradient/pallas_call | solution.py:476
  147.9 0.5 broadcast.55
  148.4 1.5 reduce.3
  149.9 0.6 reshape.45.gain_ref
  150.5 75.2 %collect.1 = (f32[1280,128]{1,0:T(8,128)}, f32[8,1024]{1,0:T(8,128)}) custom-call(bf16[8,4,1280,128]{3,2,1,0:T(8,128)(2,1)} %get-tuple-element.26.parts_ref, f32[8,1024]{1,0:T(8,128)} %reshape.45.gain_ref), custom_call_target="tpu_custom_call" | custom-call | tf_op jit(solution)/shard_map/collect/pallas_call | solution.py:505
  225.7 1.4 copy.13
  227.1 2.0 broadcast_select_fusion
  229.1 0.0 all-to-all-done
  229.1 1.5 copy.16
  (3 shorter events, 0.0 us)
Async XLA Ops:
  118.0 111.1 %all-to-all-start = ((bf16[4,128,2560]{2,1,0:T(8,128)(2,1)}), bf16[4,128,2560]{2,1,0:T(8,128)(2,1)S(1)}, u32[]{:S(2)}, u32[]{:S(2)}) async-start(bf16[4,128,2560]{2,1,0:T(8,128)(2,1)} %project.1), calls=%async_computation | async-start | bytes 5242880 | tf_op jit(solution)/shard_map/all_to_all | solution.py:475

commit v4 on v3

--- a/solution.py
+++ b/solution.py
@@ -113,8 +113,9 @@
 
                 share(q, slot)
 
-    for k in range(1, n_tensor):
-        exchange(k).start()
+        if far == 1:
+            for k in range(1, n_tensor):
+                exchange(k).start()
 
     def flip_step(i, carry):
         at = lanes(i, tile)
@@ -201,14 +202,20 @@
             device_id=to, device_id_type=MESH,
         )
 
-    def over_core(j):
+    def over_core(j, k):
         return remote(
-            parts_ref.at[near(j) * 2 + 1 - core], from_core.at[near(j)],
-            c_send.at[j], c_recv.at[j], (other, t),
-        )
-
-    def load_own(j):
-        return pltpu.make_async_copy(parts_ref.at[peer(j)], mine.at[near(j)], l_sem.at[j])
+            parts_ref.at[near(j) * 2 + 1 - core, line(k)], from_core.at[near(j), line(k)],
+            c_send.at[j, k], c_recv.at[j, k], (other, t),
+        )
+
+    def load_own(j, k):
+        return pltpu.make_async_copy(
+            parts_ref.at[peer(j), line(k)], mine.at[near(j), line(k)], l_sem.at[j, k]
+        )
+
+    def own_landed(j, k):
+        load_own(j, k).wait()
+        landed(from_core.at[near(j), line(k)], c_send.at[j, k], c_recv.at[j, k])
 
     def over_plane(j, k):
         return remote(
@@ -227,9 +234,11 @@
     order = list(range(1, pairs)) + [0]
     gain_core = remote(gain_ref, g_core, gc_send, gc_recv, (other, t))
     gain_core.start()
-    for j in order:
-        over_core(j).start()
-        load_own(j).start()
+    lines = list(range(1, n_tensor)) + [0]
+    for k in lines:
+        for j in order:
+            over_core(j, k).start()
+            load_own(j, k).start()
 
     gain_core.wait_recv()
     g_plane[pair] = gain_ref[...] + g_core[...]
@@ -242,11 +251,9 @@
 
     steps = mine.shape[2] // tile
     f32 = jnp.float32
-    lines = list(range(1, n_tensor)) + [0]
-    for j in range(1, pairs):
-        load_own(j).wait()
-        landed(from_core.at[near(j)], c_send.at[j], c_recv.at[j])
-        for k in lines:
+    for k in lines:
+        for j in range(1, pairs):
+            own_landed(j, k)
 
             def core_step(i, carry, j=j, k=k):
                 at = lanes(i, tile)
@@ -257,8 +264,6 @@
 
             lax.fori_loop(0, steps, core_step, 0)
             over_plane(j, k).start()
-    load_own(0).wait()
-    landed(from_core.at[pair], c_send.at[0], c_recv.at[0])
 
     for j in range(1, pairs):
         landed(g_plane.at[near(-j)], gp_send.at[j], gp_recv.at[j])
@@ -274,6 +279,7 @@
         copy.start()
 
     for k in lines:
+        own_landed(0, k)
         for j in range(1, pairs):
             landed(from_plane.at[near(-j), line(k)], p_send.at[j, k], p_recv.at[j, k])
 
@@ -317,9 +323,9 @@
     for copy in gain_plane + gain_line:
         copy.wait_send()
     for j in range(pairs):
-        over_core(j).wait_send()
-        if j:
-            for k in range(n_tensor):
+        for k in range(n_tensor):
+            over_core(j, k).wait_send()
+            if j:
                 over_plane(j, k).wait_send()
     for k in range(1, n_tensor):
         over_line(k).wait_send()
@@ -518,11 +524,11 @@
                 pltpu.VMEM(small, f32),
                 pltpu.VMEM((pairs,) + small, f32),
                 pltpu.VMEM((n_tensor,) + small, f32),
-                dma((pairs,)), dma((pairs,)),
+                dma((pairs, n_tensor)), dma((pairs, n_tensor)),
                 dma((pairs, n_tensor)), dma((pairs, n_tensor)),
                 dma((n_tensor,)), dma((n_tensor,)),
                 dma, dma, dma((pairs,)), dma((pairs,)), dma((n_tensor,)), dma((n_tensor,)),
-                dma((pairs,)),
+                dma((pairs, n_tensor)),
             ],
             compiler_params=pltpu.CompilerParams(
                 collective_id=1, has_side_effects=True, vmem_limit_bytes=VMEM_BYTES

time: 231 us -> 222 us (0.961)
  Pallas kernels: 212 us -> 204 us
    pallas_call x1, Pallas kernels: 75.2 us -> 68.3 us  [body(): pl.pallas_call(functools.partial(collect_kernel, pairs=pairs, n_tensor=n_...]
  transfers between devices with their start and end apart: 1 -> 1, of which waited for: 0 -> 0; matrix products, arithmetic and copies ran while one was open for 3% -> 3% of each run, Pallas kernels for 43% -> 42%
where the time goes in v4:
time: 222 us; the launch traced here: 221 us
  Pallas kernels  204 us (92%)
  other arithmetic  6.78 us (3%)
  local copies, waits for them, and re-layouts  5.04 us (2%)
  starting transfers between devices  3.65 us (2%)
    pallas_call x1, Pallas kernels, body(): pl.pallas_call(functools.partial(spread_kernel, pairs=pairs, n_tensor=n_t...  98 us
    pallas_call x1, Pallas kernels, body(): pl.pallas_call(functools.partial(collect_kernel, pairs=pairs, n_tensor=n_...  68.3 us
    pallas_call x1, Pallas kernels, body(): pl.pallas_call(functools.partial(gradient_kernel, cols=cols), out_shape=(...  24.3 us
    pallas_call x1, Pallas kernels, body(): pl.pallas_call(functools.partial(project_kernel, cols=cols), out_shape=ja...  13.4 us
  transfers between devices with their start and end apart: 1, of which 0 were waited for; matrix products, arithmetic and copies ran while one was open for 3% of the time, Pallas kernels for 42%

profile of v4, /device:TPU:0, one launch (start us, length us, event | category | flops | bytes accessed | tf_op | source)
XLA Modules:
  0.0 220.9 jit_solution(12649465043067250232)
XLA Ops:
  0.6 0.7 fusion.8
  2.0 0.1 broadcast_bitcast_fusion
  2.1 1.2 bitcast_select_fusion
  3.3 0.7 pad_maximum_fusion.tiles_ref
  4.0 98.0 %spread.1 = (bf16[8,4,1296,128]{3,2,1,0:T(8,128)(2,1)}, bf16[4,128,2560]{2,1,0:T(8,128)(2,1)}, bf16[128,8192]{1,0:T(8,128)(2,1)}, bf16[8192,128]{1,0:T(8,128)(2,...) custom-call(bf16[1296,128]{1,0:T(8,128)(2,1)} %pad_maximum_fusion.tiles_ref, bf16[4,128,2560]{2,1,0:T(8,128)(2,1)} %bitcast.17, ...), custom_call_target="tpu_custom_call" | custom-call | tf_op jit(solution)/shard_map/spread/pallas_call | solution.py:429
  102.1 1.0 copy.10
  103.0 0.6 fusion.ids_ref
  103.7 13.4 %project.1 = bf16[4,128,2560]{2,1,0:T(8,128)(2,1)} custom-call(s32[8,4,10]{2,1,0:T(4,128)} %fusion.ids_ref, bf16[128,8192]{1,0:T(8,128)(2,1)} %get-tuple-element.18.x_ref, bf16[8,4,1296,128]{3,2,1,0:T(8,128)(2,1)} %get-tuple-element.19.w_ref), custom_call_target="tpu_custom_call" | custom-call | flops 5368709120 | bytes 10485760 | tf_op jit(solution)/shard_map/project/pallas_call | solution.py:464
  117.1 3.7 %all-to-all-start = ((bf16[4,128,2560]{2,1,0:T(8,128)(2,1)}), bf16[4,128,2560]{2,1,0:T(8,128)(2,1)S(1)}, u32[]{:S(2)}, u32[]{:S(2)}) async-start(bf16[4,128,2560]{2,1,0:T(8,128)(2,1)} %project.1), calls=%async_computation | async-start | bytes 5242880 | tf_op jit(solution)/shard_map/all_to_all | solution.py:481
  120.8 24.3 %gradient.1 = (bf16[8,4,1280,128]{3,2,1,0:T(8,128)(2,1)}, bf16[128,8192]{1,0:T(8,128)(2,1)}, f32[1,8192]{1,0:T(1,128)}) custom-call(s32[8,4,10]{2,1,0:T(4,128)} %fusion.ids_ref, bf16[8192,128]{1,0:T(8,128)(2,1)} %get-tuple-element.22.xt_ref, bf16[8,4,1296,128]{3,2,1,0:T(8,128)(2,1)} %get-tuple-element.19.w_ref, ...), custom_call_target="tpu_custom_call" | custom-call | flops 10737418240 | bytes 20971520 | tf_op jit(solution)/shard_map/gradient/pallas_call | solution.py:482
  145.0 0.5 broadcast.55
  145.5 1.5 reduce.3
  147.0 0.6 reshape.45.gain_ref
  147.6 68.3 %collect.1 = (f32[1280,128]{1,0:T(8,128)}, f32[8,1024]{1,0:T(8,128)}) custom-call(bf16[8,4,1280,128]{3,2,1,0:T(8,128)(2,1)} %get-tuple-element.26.parts_ref, f32[8,1024]{1,0:T(8,128)} %reshape.45.gain_ref), custom_call_target="tpu_custom_call" | custom-call | tf_op jit(solution)/shard_map/collect/pallas_call | solution.py:511
  215.9 1.4 copy.13
  217.3 2.0 broadcast_select_fusion
  219.4 0.0 all-to-all-done
  219.4 1.5 copy.16
  (3 shorter events, 0.0 us)
Async XLA Ops:
  117.1 102.3 %all-to-all-start = ((bf16[4,128,2560]{2,1,0:T(8,128)(2,1)}), bf16[4,128,2560]{2,1,0:T(8,128)(2,1)S(1)}, u32[]{:S(2)}, u32[]{:S(2)}) async-start(bf16[4,128,2560]{2,1,0:T(8,128)(2,1)} %project.1), calls=%async_computation | async-start | bytes 5242880 | tf_op jit(solution)/shard_map/all_to_all | solution.py:481

commit v5 on v4

--- a/solution.py
+++ b/solution.py
@@ -124,12 +124,21 @@
 
     lax.fori_loop(0, width // tile, flip_step, 0)
 
-    for k in range(n_tensor):
-        q = line(-k)
+    def relay(q):
         for j in range(1, pairs):
             slot = w_ref.at[peer(-j), q]
             landed(slot, p_send.at[q, j], p_recv.at[q, j])
             over_core(q, j, slot).start()
+
+    relay(t)
+    for far in range(1, n_tensor):
+        for step in (1, -1):
+            q = t - step * far
+
+            @pl.when((q >= 0) if step > 0 else (q < n_tensor))
+            def _(q=q):
+                relay(q)
+
     for k in range(n_tensor):
         q = line(-k)
         for j in range(pairs):

time: 222 us -> 219 us (0.986)
  Pallas kernels: 204 us -> 201 us
    pallas_call x1, Pallas kernels: 98 us -> 95.2 us  [body(): pl.pallas_call(functools.partial(spread_kernel, pairs=pairs, n_tensor=n_t...]
where the time goes in v5:
time: 219 us; the launch traced here: 218 us
  Pallas kernels  201 us (92%)
  other arithmetic  6.78 us (3%)
  local copies, waits for them, and re-layouts  5.04 us (2%)
  starting transfers between devices  3.65 us (2%)
    pallas_call x1, Pallas kernels, body(): pl.pallas_call(functools.partial(spread_kernel, pairs=pairs, n_tensor=n_t...  95.2 us
    pallas_call x1, Pallas kernels, body(): pl.pallas_call(functools.partial(collect_kernel, pairs=pairs, n_tensor=n_...  68.3 us
    pallas_call x1, Pallas kernels, body(): pl.pallas_call(functools.partial(gradient_kernel, cols=cols), out_shape=(...  24.3 us
    pallas_call x1, Pallas kernels, body(): pl.pallas_call(functools.partial(project_kernel, cols=cols), out_shape=ja...  13.4 us
  transfers between devices with their start and end apart: 1, of which 0 were waited for; matrix products, arithmetic and copies ran while one was open for 3% of the time, Pallas kernels for 42%

profile of v5, /device:TPU:0, one launch (start us, length us, event | category | flops | bytes accessed | tf_op | source)
XLA Modules:
  0.0 218.0 jit_solution(711233447170848478)
XLA Ops:
  0.6 0.7 fusion.8
  2.0 0.1 broadcast_bitcast_fusion
  2.1 1.2 bitcast_select_fusion
  3.3 0.7 pad_maximum_fusion.tiles_ref
  4.0 95.2 %spread.1 = (bf16[8,4,1296,128]{3,2,1,0:T(8,128)(2,1)}, bf16[4,128,2560]{2,1,0:T(8,128)(2,1)}, bf16[128,8192]{1,0:T(8,128)(2,1)}, bf16[8192,128]{1,0:T(8,128)(2,...) custom-call(bf16[1296,128]{1,0:T(8,128)(2,1)} %pad_maximum_fusion.tiles_ref, bf16[4,128,2560]{2,1,0:T(8,128)(2,1)} %bitcast.17, ...), custom_call_target="tpu_custom_call" | custom-call | tf_op jit(solution)/shard_map/spread/pallas_call | solution.py:438
  99.2 1.0 copy.10
  100.2 0.6 fusion.ids_ref
  100.8 13.4 %project.1 = bf16[4,128,2560]{2,1,0:T(8,128)(2,1)} custom-call(s32[8,4,10]{2,1,0:T(4,128)} %fusion.ids_ref, bf16[128,8192]{1,0:T(8,128)(2,1)} %get-tuple-element.18.x_ref, bf16[8,4,1296,128]{3,2,1,0:T(8,128)(2,1)} %get-tuple-element.19.w_ref), custom_call_target="tpu_custom_call" | custom-call | flops 5368709120 | bytes 10485760 | tf_op jit(solution)/shard_map/project/pallas_call | solution.py:473
  114.2 3.7 %all-to-all-start = ((bf16[4,128,2560]{2,1,0:T(8,128)(2,1)}), bf16[4,128,2560]{2,1,0:T(8,128)(2,1)S(1)}, u32[]{:S(2)}, u32[]{:S(2)}) async-start(bf16[4,128,2560]{2,1,0:T(8,128)(2,1)} %project.1), calls=%async_computation | async-start | bytes 5242880 | tf_op jit(solution)/shard_map/all_to_all | solution.py:490
  117.9 24.3 %gradient.1 = (bf16[8,4,1280,128]{3,2,1,0:T(8,128)(2,1)}, bf16[128,8192]{1,0:T(8,128)(2,1)}, f32[1,8192]{1,0:T(1,128)}) custom-call(s32[8,4,10]{2,1,0:T(4,128)} %fusion.ids_ref, bf16[8192,128]{1,0:T(8,128)(2,1)} %get-tuple-element.22.xt_ref, bf16[8,4,1296,128]{3,2,1,0:T(8,128)(2,1)} %get-tuple-element.19.w_ref, ...), custom_call_target="tpu_custom_call" | custom-call | flops 10737418240 | bytes 20971520 | tf_op jit(solution)/shard_map/gradient/pallas_call | solution.py:491
  142.2 0.5 broadcast.55
  142.7 1.5 reduce.3
  144.2 0.6 reshape.45.gain_ref
  144.8 68.3 %collect.1 = (f32[1280,128]{1,0:T(8,128)}, f32[8,1024]{1,0:T(8,128)}) custom-call(bf16[8,4,1280,128]{3,2,1,0:T(8,128)(2,1)} %get-tuple-element.26.parts_ref, f32[8,1024]{1,0:T(8,128)} %reshape.45.gain_ref), custom_call_target="tpu_custom_call" | custom-call | tf_op jit(solution)/shard_map/collect/pallas_call | solution.py:520
  213.1 1.4 copy.13
  214.5 2.0 broadcast_select_fusion
  216.5 0.0 all-to-all-done
  216.5 1.5 copy.16
  (3 shorter events, 0.0 us)
Async XLA Ops:
  114.2 102.3 %all-to-all-start = ((bf16[4,128,2560]{2,1,0:T(8,128)(2,1)}), bf16[4,128,2560]{2,1,0:T(8,128)(2,1)S(1)}, u32[]{:S(2)}, u32[]{:S(2)}) async-start(bf16[4,128,2560]{2,1,0:T(8,128)(2,1)} %project.1), calls=%async_computation | async-start | bytes 5242880 | tf_op jit(solution)/shard_map/all_to_all | solution.py:490
